TPU v7x, 128 devices: a whole 4x4x4 slice. The times are simulated.
128 devices in a mesh: row: 16 (over x_lo, y, core), col: 8 (over x_hi, z).
Axes of the slice: x: 4 (x_hi: 2, x_lo: 2; x = x_hi * 2 + x_lo), y: 4, z: 4, core: 2. Of those that a mesh axis runs over, the one named last changes fastest.
Arguments:
- features: bfloat16 [65536, 128], P(('col', 'row')), may hold values from -6 to 6
- weight: bfloat16 [128, 256], replicated, may hold values from -0.5 to 0.5
- degrees: int32 [65536], replicated, may hold values from 8 to 32
- tile_rows: int32 [16, 8, 768], P('row', 'col'), may hold values from 0 to 31, as said below
- tile_cols: int32 [16, 8, 768], P('row', 'col'), may hold values from 0 to 63, as said below
- tile_masks: int32 [16, 8, 768, 16, 128], P('row', 'col'), may hold values from 0 to 255, as said below
- cotangent: bfloat16 [65536, 256], P(('row', 'col')), may hold values from -10 to 10
Outputs:
- activated: bfloat16 [65536, 256], P(('row', 'col'))
- grad_features: float32 [65536, 128], P(('col', 'row'))
- grad_weight: float32 [128, 256], replicated
Inputs may be any that keep to these rules, and one draw needn't show every extreme that they name: The degrees are those of the full graph, which is sparser than A; they are not A's row or column counts. `tile_rows`: each device's tiles fill its first slots; its remaining slots hold tile row 0 and tile column 0. At every grid row some device fills all 768 slots. Pairs may repeat, and repeated tiles add. `tile_cols`: empty slots hold 0. `tile_masks`: every word holds 8 bits; empty slots are all zero.
All inputs are finite; a program needn't handle non-finite values.
Results may differ from a plain program's by a relative error of at most 0.0049.
Values may be sent and summed in bfloat16 or wider, within the bound.
A program may use at most 128 MiB of HBM per device.

v0:
```python
import jax
import jax.numpy as jnp
from jax import lax
from jax.sharding import PartitionSpec as P


def unpack_tiles(mask_words):
    shifts = jnp.arange(8, dtype=jnp.int32)
    expanded = jnp.right_shift(mask_words[:, :, None, :], shifts[:, None]) & 1
    return expanded.reshape(mask_words.shape[0], 128, mask_words.shape[2]).astype(jnp.bfloat16)


def body(features, weight, degrees, tile_rows, tile_cols, tile_masks, cotangent):
    grid_row = lax.axis_index("row")
    grid_col = lax.axis_index("col")
    row_devices = lax.axis_size("row")
    col_devices = lax.axis_size("col")
    vertices = features.shape[0]
    in_width = features.shape[1]
    out_width = weight.shape[1]
    inverse = lax.rsqrt(degrees.astype(jnp.float32))
    source_scale = lax.dynamic_slice_in_dim(
        inverse, (grid_col * row_devices + grid_row) * vertices, vertices
    )
    target_scale = lax.dynamic_slice_in_dim(
        inverse, (grid_row * col_devices + grid_col) * vertices, vertices
    )
    scaled = (features.astype(jnp.float32) * source_scale[:, None]).astype(jnp.bfloat16)
    gathered = lax.all_gather(scaled, "row", axis=0, tiled=True)
    row_list = tile_rows.reshape(-1)
    col_list = tile_cols.reshape(-1)
    capacity = row_list.shape[0]
    group_size = min(128, capacity)
    rounds = capacity // group_size
    grouped = (
        row_list.reshape(rounds, group_size),
        col_list.reshape(rounds, group_size),
        tile_masks.reshape(rounds, group_size, 16, 128),
    )
    row_tiles = vertices * col_devices // 128
    col_tiles = vertices * row_devices // 128
    source_tiles = gathered.reshape(col_tiles, 128, in_width)

    def forward_step(totals, step_items):
        rows_here, cols_here, words_here = step_items
        contrib = jnp.einsum(
            "kji,kjf->kif",
            unpack_tiles(words_here),
            source_tiles[cols_here],
            preferred_element_type=jnp.float32,
        )
        return (totals.at[rows_here].add(contrib), None)

    empty_sum = jnp.zeros((row_tiles, 128, in_width), jnp.float32)
    partial_value = lax.scan(forward_step, empty_sum, grouped)[0].reshape(row_tiles * 128, in_width)
    summed = lax.psum_scatter(partial_value, "col", scatter_dimension=0, tiled=True)
    aggregated = summed * target_scale[:, None]
    weight_full = weight.astype(jnp.float32)
    pre_act = jnp.dot(aggregated, weight_full, precision=lax.Precision.HIGHEST)
    activated = jax.nn.elu(pre_act).astype(jnp.bfloat16)
    slope_factor = jnp.where(
        pre_act > 0, jnp.ones_like(pre_act), jnp.exp(jnp.minimum(pre_act, 0.0))
    )
    pre_grad = cotangent.astype(jnp.float32) * slope_factor
    node_total = vertices * row_devices * col_devices
    grad_part = jnp.dot(aggregated.T, pre_grad, precision=lax.Precision.HIGHEST) * node_total ** (
        -0.5
    )
    grad_weight = lax.psum(grad_part, ("row", "col"))
    scaled_grad = (pre_grad * target_scale[:, None]).astype(jnp.bfloat16)
    gathered_rows = lax.all_gather(scaled_grad, "col", axis=0, tiled=True)
    target_tiles = gathered_rows.reshape(row_tiles, 128, out_width)

    def backward_step(totals, step_items):
        rows_here, cols_here, words_here = step_items
        contrib = jnp.einsum(
            "kji,kif->kjf",
            unpack_tiles(words_here),
            target_tiles[rows_here],
            preferred_element_type=jnp.float32,
        )
        return (totals.at[cols_here].add(contrib), None)

    empty_back = jnp.zeros((col_tiles, 128, out_width), jnp.float32)
    partial_back = lax.scan(backward_step, empty_back, grouped)[0].reshape(
        col_tiles * 128, out_width
    )
    weight_back = weight_full.T
    transposed = lax.psum_scatter(partial_back, "row", scatter_dimension=0, tiled=True)
    projected = jnp.dot(transposed, weight_back, precision=lax.Precision.HIGHEST)
    grad_features = projected * source_scale[:, None]
    return (activated, grad_features, grad_weight)


def solution(mesh):
    in_specs = (
        P(("col", "row"), None),
        P(),
        P(),
        P("row", "col", None),
        P("row", "col", None),
        P("row", "col", None, None, None),
        P(("row", "col"), None),
    )
    out_specs = (P(("row", "col"), None), P(("col", "row"), None), P())
    return jax.shard_map(body, mesh=mesh, in_specs=in_specs, out_specs=out_specs, check_vma=False)
```

profile of v0, /device:TPU:1, one launch (start us, length us, event | category | flops | bytes accessed | tf_op | source)
XLA Modules:
  0.0 940.8 jit_solution(16648170540121313977)
XLA Ops:
  7.2 1.0 convert_rsqrt_fusion
  8.9 1.7 multiply_convert_fusion.1
  12.1 36.4 %all-gather.3.cloned.1.call-done = bf16[8192,128]{1,0:T(8,128)(2,1)} async-done(((bf16[512,128]{1,0:T(8,128)(2,1)}), bf16[8192,128]{1,0:T(8,128)(2,1)}) %all-gather.3.cloned.1.call-update) | async-done | bytes 2097168 | tf_op jit(solution)/shard_map/all_gather | solution.py:29
  48.7 181.3 %while.20 = (s32[]{:T(128)}, f32[32,128,128]{2,1,0:T(8,128)S(1)}, s32[6,128]{1,0:T(8,128)S(1)}, s32[6,128,16,128]{3,2,1,0:T(8,128)}, s32[6,128]{1,0:T(8,128)S(1)}, /*index=5*/bf16[64,128,128]{2,1,0:T(8,128)(2,1)}, s32[]{:T(128)}) while((s32[]{:T(128)}, f32[32,128,128]{2,1,0:T(8,128)S(1)}, s32[6,128]{1,0:T(8,128)S(1)}, ...), condition=%wide.region_2.3_spmd, body=%wide.region_0.2_spmd.sunk | while | flops 545261312 | bytes 49292892 | solution.py:55
  48.8 1.3 dynamic-slice_bitcast_fusion.4
  50.1 4.6 gather_fusion
  54.8 7.1 fusion.52
  61.9 17.1 %scatter_fusion = f32[32,128,128]{2,1,0:T(8,128)S(1)} fusion(f32[32,128,128]{2,1,0:T(8,128)S(1)} %get-tuple-element.198, s32[128]{0:T(128)S(1)} %get-tuple-element.180, f32[128,128,128]{2,1,0:T(8,128)} %fusion.52), kind=kCustom, calls=%fused_computation.2.clone.1 | custom fusion | flops 2097152 | bytes 25166336 | tf_op jit(solution)/shard_map/while/body/eval_jaxpr/scatter-add | solution.py:52
  79.1 1.3 dynamic-slice_bitcast_fusion.4
  80.4 4.6 gather_fusion
  85.0 7.1 fusion.52
  92.1 17.0 %scatter_fusion = f32[32,128,128]{2,1,0:T(8,128)S(1)} fusion(f32[32,128,128]{2,1,0:T(8,128)S(1)} %get-tuple-element.198, s32[128]{0:T(128)S(1)} %get-tuple-element.180, f32[128,128,128]{2,1,0:T(8,128)} %fusion.52), kind=kCustom, calls=%fused_computation.2.clone.1 | custom fusion | flops 2097152 | bytes 25166336 | tf_op jit(solution)/shard_map/while/body/eval_jaxpr/scatter-add | solution.py:52
  109.3 1.3 dynamic-slice_bitcast_fusion.4
  110.6 4.6 gather_fusion
  115.2 7.1 fusion.52
  122.3 17.0 %scatter_fusion = f32[32,128,128]{2,1,0:T(8,128)S(1)} fusion(f32[32,128,128]{2,1,0:T(8,128)S(1)} %get-tuple-element.198, s32[128]{0:T(128)S(1)} %get-tuple-element.180, f32[128,128,128]{2,1,0:T(8,128)} %fusion.52), kind=kCustom, calls=%fused_computation.2.clone.1 | custom fusion | flops 2097152 | bytes 25166336 | tf_op jit(solution)/shard_map/while/body/eval_jaxpr/scatter-add | solution.py:52
  139.5 1.3 dynamic-slice_bitcast_fusion.4
  140.8 4.6 gather_fusion
  145.4 7.1 fusion.52
  152.5 17.0 %scatter_fusion = f32[32,128,128]{2,1,0:T(8,128)S(1)} fusion(f32[32,128,128]{2,1,0:T(8,128)S(1)} %get-tuple-element.198, s32[128]{0:T(128)S(1)} %get-tuple-element.180, f32[128,128,128]{2,1,0:T(8,128)} %fusion.52), kind=kCustom, calls=%fused_computation.2.clone.1 | custom fusion | flops 2097152 | bytes 25166336 | tf_op jit(solution)/shard_map/while/body/eval_jaxpr/scatter-add | solution.py:52
  169.7 1.3 dynamic-slice_bitcast_fusion.4
  171.0 4.6 gather_fusion
  175.6 7.1 fusion.52
  182.7 17.0 %scatter_fusion = f32[32,128,128]{2,1,0:T(8,128)S(1)} fusion(f32[32,128,128]{2,1,0:T(8,128)S(1)} %get-tuple-element.198, s32[128]{0:T(128)S(1)} %get-tuple-element.180, f32[128,128,128]{2,1,0:T(8,128)} %fusion.52), kind=kCustom, calls=%fused_computation.2.clone.1 | custom fusion | flops 2097152 | bytes 25166336 | tf_op jit(solution)/shard_map/while/body/eval_jaxpr/scatter-add | solution.py:52
  199.9 1.3 dynamic-slice_bitcast_fusion.4
  201.2 4.6 gather_fusion
  205.8 7.1 fusion.52
  212.9 17.0 %scatter_fusion = f32[32,128,128]{2,1,0:T(8,128)S(1)} fusion(f32[32,128,128]{2,1,0:T(8,128)S(1)} %get-tuple-element.198, s32[128]{0:T(128)S(1)} %get-tuple-element.180, f32[128,128,128]{2,1,0:T(8,128)} %fusion.52), kind=kCustom, calls=%fused_computation.2.clone.1 | custom fusion | flops 2097152 | bytes 25166336 | tf_op jit(solution)/shard_map/while/body/eval_jaxpr/scatter-add | solution.py:52
  229.9 1.3 copy-done.1
  231.3 73.5 %reduce-scatter.3.cloned.1.call-done = f32[512,128]{1,0:T(8,128)} async-done(((f32[4096,128]{1,0:T(8,128)}), f32[512,128]{1,0:T(8,128)}) %reduce-scatter.3.cloned.1.call-update) | async-done | bytes 262160 | tf_op jit(solution)/shard_map/reduce_scatter | solution.py:56
  304.8 2.5 multiply_convert_fusion
  307.4 54.2 %all-gather.5.cloned.1.call-done = bf16[4096,256]{1,0:T(8,128)(2,1)} async-done(((bf16[512,256]{1,0:T(8,128)(2,1)}), bf16[4096,256]{1,0:T(8,128)(2,1)}) %all-gather.5.cloned.1.call-update) | async-done | bytes 2097168 | tf_op jit(solution)/shard_map/all_gather | solution.py:71
  361.6 4.2 broadcast_in_dim.13
  365.9 350.1 %while.21 = (s32[]{:T(128)}, f32[64,128,256]{2,1,0:T(8,128)}, s32[6,128]{1,0:T(8,128)S(1)}, s32[6,128,16,128]{3,2,1,0:T(8,128)}, s32[6,128]{1,0:T(8,128)S(1)}, /*index=5*/bf16[32,128,256]{2,1,0:T(8,128)(2,1)S(1)}, s32[]{:T(128)}) while((s32[]{:T(128)}, f32[64,128,256]{2,1,0:T(8,128)}, s32[6,128]{1,0:T(8,128)S(1)}, ...), condition=%wide.region_6.7_spmd, body=%wide.region_4.6_spmd.sunk | while | flops 1084229376 | bytes 95430240 | solution.py:85
  366.0 1.3 dynamic-slice_bitcast_fusion.5
  367.3 6.6 gather_fusion.1
  373.9 11.5 %fusion.56 = f32[128,128,256]{2,1,0:T(8,128)} fusion(bf16[128,128,256]{2,1,0:T(8,128)(2,1)} %gather_fusion.1, s32[128]{0:T(128)S(1)} %shift_right_arithmetic.91, s32[128,16,128]{2,1,0:T(8,128)S(1)} %dynamic-slice_bitcast_fusion.5), kind=kOutput, calls=%fused_computation.25.clone.1 | convolution fusion | flops 1080033280 | bytes 26214912 | tf_op jit(solution)/shard_map/while/body/eval_jaxpr/kji,kif->kjf/dot_general | solution.py:76
  385.4 38.5 %scatter_fusion.1 = f32[64,128,256]{2,1,0:T(8,128)} fusion(f32[64,128,256]{2,1,0:T(8,128)} %get-tuple-element.219, s32[128]{0:T(128)S(1)} %get-tuple-element.188, f32[128,128,256]{2,1,0:T(8,128)} %fusion.56), kind=kCustom, calls=%fused_computation.3.clone.1 | custom fusion | flops 4194304 | bytes 50332160 | tf_op jit(solution)/shard_map/while/body/eval_jaxpr/scatter-add | solution.py:82
  424.0 1.3 dynamic-slice_bitcast_fusion.5
  425.3 6.5 gather_fusion.1
  431.8 11.5 %fusion.56 = f32[128,128,256]{2,1,0:T(8,128)} fusion(bf16[128,128,256]{2,1,0:T(8,128)(2,1)} %gather_fusion.1, s32[128]{0:T(128)S(1)} %shift_right_arithmetic.91, s32[128,16,128]{2,1,0:T(8,128)S(1)} %dynamic-slice_bitcast_fusion.5), kind=kOutput, calls=%fused_computation.25.clone.1 | convolution fusion | flops 1080033280 | bytes 26214912 | tf_op jit(solution)/shard_map/while/body/eval_jaxpr/kji,kif->kjf/dot_general | solution.py:76
  443.3 39.0 %scatter_fusion.1 = f32[64,128,256]{2,1,0:T(8,128)} fusion(f32[64,128,256]{2,1,0:T(8,128)} %get-tuple-element.219, s32[128]{0:T(128)S(1)} %get-tuple-element.188, f32[128,128,256]{2,1,0:T(8,128)} %fusion.56), kind=kCustom, calls=%fused_computation.3.clone.1 | custom fusion | flops 4194304 | bytes 50332160 | tf_op jit(solution)/shard_map/while/body/eval_jaxpr/scatter-add | solution.py:82
  482.4 1.3 dynamic-slice_bitcast_fusion.5
  483.7 6.2 gather_fusion.1
  489.9 11.5 %fusion.56 = f32[128,128,256]{2,1,0:T(8,128)} fusion(bf16[128,128,256]{2,1,0:T(8,128)(2,1)} %gather_fusion.1, s32[128]{0:T(128)S(1)} %shift_right_arithmetic.91, s32[128,16,128]{2,1,0:T(8,128)S(1)} %dynamic-slice_bitcast_fusion.5), kind=kOutput, calls=%fused_computation.25.clone.1 | convolution fusion | flops 1080033280 | bytes 26214912 | tf_op jit(solution)/shard_map/while/body/eval_jaxpr/kji,kif->kjf/dot_general | solution.py:76
  501.4 39.3 %scatter_fusion.1 = f32[64,128,256]{2,1,0:T(8,128)} fusion(f32[64,128,256]{2,1,0:T(8,128)} %get-tuple-element.219, s32[128]{0:T(128)S(1)} %get-tuple-element.188, f32[128,128,256]{2,1,0:T(8,128)} %fusion.56), kind=kCustom, calls=%fused_computation.3.clone.1 | custom fusion | flops 4194304 | bytes 50332160 | tf_op jit(solution)/shard_map/while/body/eval_jaxpr/scatter-add | solution.py:82
  540.8 1.3 dynamic-slice_bitcast_fusion.5
  542.1 6.2 gather_fusion.1
  548.3 11.5 %fusion.56 = f32[128,128,256]{2,1,0:T(8,128)} fusion(bf16[128,128,256]{2,1,0:T(8,128)(2,1)} %gather_fusion.1, s32[128]{0:T(128)S(1)} %shift_right_arithmetic.91, s32[128,16,128]{2,1,0:T(8,128)S(1)} %dynamic-slice_bitcast_fusion.5), kind=kOutput, calls=%fused_computation.25.clone.1 | convolution fusion | flops 1080033280 | bytes 26214912 | tf_op jit(solution)/shard_map/while/body/eval_jaxpr/kji,kif->kjf/dot_general | solution.py:76
  559.9 39.3 %scatter_fusion.1 = f32[64,128,256]{2,1,0:T(8,128)} fusion(f32[64,128,256]{2,1,0:T(8,128)} %get-tuple-element.219, s32[128]{0:T(128)S(1)} %get-tuple-element.188, f32[128,128,256]{2,1,0:T(8,128)} %fusion.56), kind=kCustom, calls=%fused_computation.3.clone.1 | custom fusion | flops 4194304 | bytes 50332160 | tf_op jit(solution)/shard_map/while/body/eval_jaxpr/scatter-add | solution.py:82
  599.2 1.3 dynamic-slice_bitcast_fusion.5
  600.5 6.2 gather_fusion.1
  606.8 11.5 %fusion.56 = f32[128,128,256]{2,1,0:T(8,128)} fusion(bf16[128,128,256]{2,1,0:T(8,128)(2,1)} %gather_fusion.1, s32[128]{0:T(128)S(1)} %shift_right_arithmetic.91, s32[128,16,128]{2,1,0:T(8,128)S(1)} %dynamic-slice_bitcast_fusion.5), kind=kOutput, calls=%fused_computation.25.clone.1 | convolution fusion | flops 1080033280 | bytes 26214912 | tf_op jit(solution)/shard_map/while/body/eval_jaxpr/kji,kif->kjf/dot_general | solution.py:76
  618.3 39.3 %scatter_fusion.1 = f32[64,128,256]{2,1,0:T(8,128)} fusion(f32[64,128,256]{2,1,0:T(8,128)} %get-tuple-element.219, s32[128]{0:T(128)S(1)} %get-tuple-element.188, f32[128,128,256]{2,1,0:T(8,128)} %fusion.56), kind=kCustom, calls=%fused_computation.3.clone.1 | custom fusion | flops 4194304 | bytes 50332160 | tf_op jit(solution)/shard_map/while/body/eval_jaxpr/scatter-add | solution.py:82
  657.7 1.3 dynamic-slice_bitcast_fusion.5
  659.0 6.2 gather_fusion.1
  665.2 11.5 %fusion.56 = f32[128,128,256]{2,1,0:T(8,128)} fusion(bf16[128,128,256]{2,1,0:T(8,128)(2,1)} %gather_fusion.1, s32[128]{0:T(128)S(1)} %shift_right_arithmetic.91, s32[128,16,128]{2,1,0:T(8,128)S(1)} %dynamic-slice_bitcast_fusion.5), kind=kOutput, calls=%fused_computation.25.clone.1 | convolution fusion | flops 1080033280 | bytes 26214912 | tf_op jit(solution)/shard_map/while/body/eval_jaxpr/kji,kif->kjf/dot_general | solution.py:76
  676.7 39.3 %scatter_fusion.1 = f32[64,128,256]{2,1,0:T(8,128)} fusion(f32[64,128,256]{2,1,0:T(8,128)} %get-tuple-element.219, s32[128]{0:T(128)S(1)} %get-tuple-element.188, f32[128,128,256]{2,1,0:T(8,128)} %fusion.56), kind=kCustom, calls=%fused_computation.3.clone.1 | custom fusion | flops 4194304 | bytes 50332160 | tf_op jit(solution)/shard_map/while/body/eval_jaxpr/scatter-add | solution.py:82
  716.1 0.9 copy-done.3
  717.2 1.4 convolution_multiply_fusion.1
  718.6 66.5 %reduce-scatter.5.cloned.1.call-done = f32[512,256]{1,0:T(8,128)} async-done(((f32[8192,256]{1,0:T(8,128)}), f32[512,256]{1,0:T(8,128)}) %reduce-scatter.5.cloned.1.call-update) | async-done | bytes 524304 | tf_op jit(solution)/shard_map/reduce_scatter | solution.py:89
  785.1 2.1 convolution_multiply_fusion
  787.2 145.5 %all-reduce.2.cloned.1.call-done = f32[128,256]{1,0:T(8,128)} async-done(((f32[128,256]{1,0:T(8,128)}), f32[128,256]{1,0:T(8,128)}) %all-reduce.2.cloned.1.call-update) | async-done | bytes 131088 | tf_op jit(solution)/shard_map/psum | solution.py:69
  932.7 1.6 copy.30
  (82 shorter events, 4.0 us)
Async XLA Ops:
  7.2 297.6 %copy-start = (bf16[128,256]{1,0:T(8,128)(2,1)S(1)}, bf16[128,256]{1,0:T(8,128)(2,1)}, u32[]{:S(2)}) copy-start(bf16[128,256]{1,0:T(8,128)(2,1)} %param.12) | copy-start | bytes 196612
  7.2 41.2 %all-gather.3.cloned.1.call-start = ((), (), s32[]{:S(2)}) async-start(), calls=%async_computation.2 | async-start | bytes 2228224 | tf_op jit(solution)/shard_map/all_gather | solution.py:29
  8.3 0.6 copy-start.7
  8.3 296.5 %copy-start.9 = (f32[512]{0:T(512)}, f32[512]{0:T(512)S(1)}, u32[]{:S(2)}) copy-start(f32[512]{0:T(512)S(1)} %get-tuple-element.105) | copy-start | bytes 6148
  10.6 294.2 %reduce-scatter.3.cloned.1.call-start = ((), (), s32[]{:S(2)}) async-start(), calls=%async_computation.3 | async-start | bytes 2359296 | tf_op jit(solution)/shard_map/reduce_scatter | solution.py:56
  48.7 256.1 %copy-start.4 = (bf16[512,256]{1,0:T(8,128)(2,1)S(1)}, bf16[512,256]{1,0:T(8,128)(2,1)}, u32[]{:S(2)}) copy-start(bf16[512,256]{1,0:T(8,128)(2,1)} %param.17) | copy-start | bytes 786436
  229.9 1.3 copy-start.1
  231.3 130.3 %all-gather.5.cloned.1.call-start = ((), (), s32[]{:S(2)}) async-start(), calls=%async_computation.4 | async-start | bytes 2359296 | tf_op jit(solution)/shard_map/all_gather | solution.py:71
  307.4 477.7 %reduce-scatter.5.cloned.1.call-start = ((), (), s32[]{:S(2)}) async-start(), calls=%async_computation.5 | async-start | bytes 8912896 | tf_op jit(solution)/shard_map/reduce_scatter | solution.py:89
  361.6 4.2 copy-start.2
  716.0 1.0 copy-start.3
  716.0 1.1 copy-start.5
  716.0 1.2 copy-start.6
  716.0 1.2 copy-start.10
  716.0 69.0 %copy-start.8 = (f32[512]{0:T(512)S(1)}, f32[512]{0:T(512)}, u32[]{:S(2)}) copy-start(f32[512]{0:T(512)} %copy-done.7) | copy-start | bytes 6148
  716.0 216.7 %all-reduce.2.cloned.1.call-start = ((), (), s32[]{:S(2)}) async-start(), calls=%async_computation.6 | async-start | bytes 262144 | tf_op jit(solution)/shard_map/psum | solution.py:69
Sparse Core Ops, SparseCore 0:
  10.7 37.6 all-gather.2
  231.4 73.3 reduce-scatter.2
  307.7 53.8 all-gather.4
  716.2 68.8 reduce-scatter.4
  790.2 142.4 all-reduce.1
where the time goes:
time: 944 us; the launch traced here: 941 us
  waiting for transfers between devices  376 us (40%)
  other arithmetic  341 us (36%)
  matrix products  118 us (12%)
  local copies, waits for them, and re-layouts  91.6 us (10%)
  between operations  13.9 us (1%)
    scatter-add x6, other arithmetic, backward_step(): return (totals.at[cols_here].add(contrib), None)  235 us
    psum x1, waiting for transfers between devices, body(): grad_weight = lax.psum(grad_part, ('row', 'col'))  146 us
    scatter-add x6, other arithmetic, forward_step(): return (totals.at[rows_here].add(contrib), None)  102 us
    reduce_scatter x1, waiting for transfers between devices, body(): lax.psum_scatter(partial_value, 'col', scatter_dimension=0, tiled=True)  73.5 us
    dot_general x6, matrix products, backward_step(): jnp.einsum('kji,kif->kjf', unpack_tiles(words_here), target_tiles[rows_he...  69.1 us
    reduce_scatter x1, waiting for transfers between devices, body(): lax.psum_scatter(partial_back, 'row', scatter_dimension=0, tiled=True)  66.5 us
    all_gather x1, waiting for transfers between devices, body(): gathered_rows = lax.all_gather(scaled_grad, 'col', axis=0, tiled=True)  54.2 us
    dot_general x6, matrix products, forward_step(): jnp.einsum('kji,kjf->kif', unpack_tiles(words_here), source_tiles[cols_he...  42.6 us
  transfers between devices with their start and end apart: 5, of which 5 were waited for; matrix products, arithmetic and copies ran while one was open for 1% of the time, Pallas kernels for 0%

commit v1 on v0

v1 whole, which is shorter than its diff:
```python
import functools

import jax
import jax.numpy as jnp
from jax import lax
from jax.experimental import pallas as pl
from jax.experimental.pallas import tpu as pltpu
from jax.sharding import PartitionSpec as P

F32 = jnp.float32
BF16 = jnp.bfloat16
I32 = jnp.int32
MESH = pl.DeviceIdType.MESH
VMEM = pltpu.VMEM
SLOTS = 1024
ROW_BITS = 5
COL_BITS = 6
CODE_BITS = ROW_BITS + COL_BITS
FWD_GROUP, FWD_UNROLL = 4, 4
BWD_GROUP, BWD_UNROLL = 4, 4
BIG = 48 * 1024 * 1024


def mm(a, b):
    return jnp.dot(a, b, preferred_element_type=F32)


def iota(shape, dim):
    return lax.broadcasted_iota(I32, shape, dim)


def split(x):
    hi = x.astype(BF16)
    return hi, (x - hi.astype(F32)).astype(BF16)


def greet(axis, count):
    me = lax.axis_index(axis)
    barrier = pltpu.get_barrier_semaphore()
    for step in range(1, count):
        peer = lax.rem(me + step, count)
        pl.semaphore_signal(barrier, inc=1, device_id={axis: peer}, device_id_type=MESH)
    pl.semaphore_wait(barrier, count - 1)


def order_list(keys, rows, cols, n_keys, group):
    cap = keys.shape[1]
    hot = iota((n_keys, cap), 0) == keys
    hot_f = hot.astype(F32)
    upper = (iota((cap, cap), 0) < iota((cap, cap), 1)).astype(F32).astype(BF16)
    rank = mm(hot_f.astype(BF16), upper)
    count = jnp.sum(hot_f, axis=1, keepdims=True)
    groups = jnp.floor((count + (group - 1)) * (1.0 / group))
    wide = jnp.broadcast_to(groups, (n_keys, 128)).astype(BF16)
    lower = (iota((n_keys, n_keys), 1) < iota((n_keys, n_keys), 0)).astype(F32).astype(BF16)
    base = mm(lower, wide)[:, :1] * group
    pos = jnp.sum(hot_f * (rank + base), axis=0, keepdims=True)
    place = (iota((SLOTS, cap), 0) == pos.astype(I32)).astype(F32).astype(BF16)
    which = iota((8, cap), 0)
    slot = iota((8, cap), 1)
    vals = jnp.where(
        which == 0,
        slot >> 4,
        jnp.where(
            which == 1,
            slot & 15,
            jnp.where(which == 2, cols, jnp.where(which == 3, rows, jnp.where(which == 4, 1, 0))),
        ),
    )
    vals = vals.astype(F32).astype(BF16)
    found = lax.dot_general(vals, place, (((1,), (1,)), ((), ())), preferred_element_type=F32)
    f = found.astype(I32)
    code = ((f[0:1] * 16 + f[1:2]) << CODE_BITS) | (f[2:3] << ROW_BITS) | f[3:4]
    code = jnp.where(f[4:5] > 0, code, cap << CODE_BITS)
    total = jnp.sum(groups, axis=0, keepdims=True).astype(I32)
    return jnp.where(iota((8, SLOTS), 0) == 0, code, total)


def gather_kernel(n, feat, deg, rows, cols, out, fwd_list, bwd_list, mine, send_sem, recv_sem, own_sem):
    me = lax.axis_index("row")
    lane = iota((128, 128), 1)
    perm = (iota((128, 128), 0) == ((lane & 15) * 8 + (lane >> 4))).astype(F32).astype(BF16)
    degrees = mm(deg[...].astype(F32).astype(BF16), perm)
    bucket = iota((1, 128), 1) >> 4
    shrink = jnp.zeros((1, 128), F32)
    for b in range(8):
        shrink = jnp.where(bucket == b, 2.0**-b, shrink)
    inverse = lax.rsqrt(degrees)
    for t in range(4):
        turned = lax.dot_general(
            feat[t * 128 : (t + 1) * 128, :], perm, (((0,), (0,)), ((), ())), preferred_element_type=F32
        )
        mine[t] = (turned * inverse[t : t + 1, :] * shrink).astype(BF16)
    greet("row", n)
    copies = []
    here = out.at[pl.ds(me * 4, 4)]
    for step in range(1, n):
        peer = lax.rem(me + step, n)
        copy = pltpu.make_async_remote_copy(
            src_ref=mine,
            dst_ref=here,
            send_sem=send_sem.at[step],
            recv_sem=recv_sem.at[step],
            device_id={"row": peer},
            device_id_type=MESH,
        )
        copy.start()
        copies.append(copy)
    own = pltpu.make_async_copy(mine, here, own_sem)
    own.start()
    r, c = rows[...], cols[...]
    fwd_list[...] = order_list(r, r, c, 1 << ROW_BITS, FWD_GROUP)
    bwd_list[...] = order_list(c, r, c, 1 << COL_BITS, BWD_GROUP)
    own.wait()
    for copy in copies:
        copy.wait()


def unpack(words):
    return [(words & (1 << b)).astype(F32).astype(BF16) for b in range(8)]


def load_masks(masks, held, sem):
    copy = pltpu.make_async_copy(masks, held.at[pl.ds(0, 768)], sem)
    copy.start()
    held[768] = jnp.zeros((16, 128), I32)
    return copy


def forward_kernel(codes, src, masks, out, held, acc, sem):
    copy = load_masks(masks, held, sem)
    acc[...] = jnp.zeros_like(acc)
    copy.wait()
    group, unroll = FWD_GROUP, FWD_UNROLL

    def body(i, carry):
        for u in range(unroll):
            at = (i * unroll + u) * group
            code = [codes[0, at + g] for g in range(group)]
            target = code[0] & ((1 << ROW_BITS) - 1)
            lhs = jnp.concatenate(
                [src[(k >> ROW_BITS) & ((1 << COL_BITS) - 1)] for k in code], axis=1
            )
            rhs = jnp.concatenate(
                [part for k in code for part in unpack(held[k >> CODE_BITS])], axis=0
            )
            acc[target] += mm(lhs, rhs)
        return carry

    lax.fori_loop(0, (codes[1, 0] + unroll - 1) // unroll, body, 0)
    out[...] = acc[...].astype(BF16)


def backward_kernel(codes, src, masks, out, held, acc, sem):
    copy = load_masks(masks, held, sem)
    acc[...] = jnp.zeros_like(acc)
    copy.wait()
    group, unroll = BWD_GROUP, BWD_UNROLL

    def body(i, carry):
        for u in range(unroll):
            at = (i * unroll + u) * group
            code = [codes[0, at + g] for g in range(group)]
            target = (code[0] >> ROW_BITS) & ((1 << COL_BITS) - 1)
            rhs = jnp.concatenate([src[k & ((1 << ROW_BITS) - 1)] for k in code], axis=0)
            lhs = jnp.concatenate(
                [jnp.concatenate(unpack(held[k >> CODE_BITS]), axis=0) for k in code], axis=1
            )
            acc[target] += mm(lhs, rhs)
        return carry

    lax.fori_loop(0, (codes[1, 0] + unroll - 1) // unroll, body, 0)
    out[...] = acc[...].astype(BF16)


def layer_kernel(n, scale, part, weight, deg, cot, act, out, gw, got, mine, s1, r1, s2, r2, own1, own2):
    me = lax.axis_index("col")
    greet("col", n)
    copies = []
    for step in range(1, n):
        peer = lax.rem(me + step, n)
        copy = pltpu.make_async_remote_copy(
            src_ref=part.at[pl.ds(peer * 4, 4)],
            dst_ref=got.at[step],
            send_sem=s1.at[step],
            recv_sem=r1.at[step],
            device_id={"col": peer},
            device_id_type=MESH,
        )
        copy.start()
        copies.append(copy)
    own = pltpu.make_async_copy(part.at[pl.ds(me * 4, 4)], got.at[0], own1)
    own.start()
    own.wait()
    for copy in copies:
        copy.wait()
    w = weight[...]
    inverse = lax.rsqrt(deg[...].astype(F32))
    total = jnp.zeros((128, 256), F32)
    for t in range(4):
        summed = got[0, t].astype(F32)
        for step in range(1, n):
            summed = summed + got[step, t].astype(F32)
        factor = jnp.broadcast_to(inverse[t : t + 1, :], (128, 128))
        agg_t = summed * factor
        factor = factor.T
        factor = jnp.concatenate([factor, factor], axis=1)
        t_hi, t_lo = split(agg_t)
        hi, lo = split(agg_t.T)
        pre = mm(hi, w) + mm(lo, w)
        slope = jnp.where(pre > 0, 1.0, jnp.exp(jnp.minimum(pre, 0.0)))
        rows = pl.ds(t * 128, 128)
        act[rows, :] = jnp.where(pre > 0, pre, slope - 1.0).astype(BF16)
        grad = cot[rows, :].astype(F32) * slope
        g_hi, g_lo = split(grad)
        total = total + (mm(t_hi, g_hi) + (mm(t_lo, g_hi) + mm(t_hi, g_lo)))
        scaled = (grad * factor).astype(BF16)
        mine[t] = lax.dot_general(
            scaled, w, (((1,), (1,)), ((), ())), preferred_element_type=F32
        ).astype(BF16)
    here = out.at[pl.ds(me * 4, 4)]
    copies = []
    for step in range(1, n):
        peer = lax.rem(me + step, n)
        copy = pltpu.make_async_remote_copy(
            src_ref=mine,
            dst_ref=here,
            send_sem=s2.at[step],
            recv_sem=r2.at[step],
            device_id={"col": peer},
            device_id_type=MESH,
        )
        copy.start()
        copies.append(copy)
    own = pltpu.make_async_copy(mine, here, own2)
    own.start()
    gw[...] = total * scale
    own.wait()
    for copy in copies:
        copy.wait()


def finish_kernel(
    n_row, n_col, part, deg, gw, out, gw_out, got, gw_got, gw_row, gw_col, gw_all,
    s1, r1, s2, r2, s3, r3, s4, r4, own_sem,
):
    row = lax.axis_index("row")
    col = lax.axis_index("col")
    barrier = pltpu.get_barrier_semaphore()
    for step in range(1, n_row):
        pl.semaphore_signal(
            barrier, inc=1, device_id={"row": lax.rem(row + step, n_row)}, device_id_type=MESH
        )
    for step in range(1, n_col):
        pl.semaphore_signal(
            barrier, inc=1, device_id={"col": lax.rem(col + step, n_col)}, device_id_type=MESH
        )
    pl.semaphore_wait(barrier, n_row + n_col - 2)

    def send(src, dst, sems, step, axis, me, count):
        copy = pltpu.make_async_remote_copy(
            src_ref=src,
            dst_ref=dst,
            send_sem=sems[0].at[step],
            recv_sem=sems[1].at[step],
            device_id={axis: lax.rem(me + step, count)},
            device_id_type=MESH,
        )
        copy.start()
        return copy

    weights = []
    for step in range(1, n_row):
        peer = lax.rem(row + step, n_row)
        weights.append(
            send(gw.at[pl.ds(peer * 8, 8)], gw_got.at[step], (s2, r2), step, "row", row, n_row)
        )
    main = []
    for step in range(1, n_row):
        peer = lax.rem(row + step, n_row)
        main.append(
            send(part.at[pl.ds(peer * 4, 4)], got.at[step], (s1, r1), step, "row", row, n_row)
        )
    own = pltpu.make_async_copy(part.at[pl.ds(row * 4, 4)], got.at[0], own_sem)
    own.start()
    for copy in weights:
        copy.wait()
    summed = gw[pl.ds(row * 8, 8), :]
    for step in range(1, n_row):
        summed = summed + gw_got[step]
    gw_row[...] = summed
    gw_col[pl.ds(col, 1)] = summed[None]
    weights = [
        send(gw_row, gw_col.at[col], (s3, r3), step, "col", col, n_col) for step in range(1, n_col)
    ]
    for copy in weights:
        copy.wait()
    summed = gw_col[0]
    for c in range(1, n_col):
        summed = summed + gw_col[c]
    mine = gw_all.at[pl.ds(row * 8, 8)]
    gw_all[pl.ds(row * 8, 8), :] = summed
    weights = [send(mine, mine, (s4, r4), step, "row", row, n_row) for step in range(1, n_row)]
    inverse = lax.rsqrt(deg[...].astype(F32))
    own.wait()
    for copy in main:
        copy.wait()
    for t in range(4):
        factor = jnp.broadcast_to(inverse[t : t + 1, :], (128, 128)).T
        for b in range(8):
            total = got[0, t, b * 16 : (b + 1) * 16, :].astype(F32)
            for step in range(1, n_row):
                total = total + got[step, t, b * 16 : (b + 1) * 16, :].astype(F32)
            out[pl.ds(t * 128 + b, 16, stride=8), :] = total * (2.0**-b)
        rows = pl.ds(t * 128, 128)
        out[rows, :] = out[rows, :] * factor
    for copy in weights:
        copy.wait()
    gw_out[...] = gw_all[...]


def spec(space=VMEM):
    return pl.BlockSpec(memory_space=space)


def shaped(shape, dtype):
    return jax.ShapeDtypeStruct(shape, dtype)


def remote_params(number):
    return pltpu.CompilerParams(
        collective_id=number, has_side_effects=True, vmem_limit_bytes=BIG
    )


def dma(count):
    return pltpu.SemaphoreType.DMA((count,))


def body(features, weight, degrees, tile_rows, tile_cols, tile_masks, cotangent):
    row = lax.axis_index("row")
    col = lax.axis_index("col")
    n_row = lax.axis_size("row")
    n_col = lax.axis_size("col")
    deg = degrees.reshape(n_row * n_col, 4, 128)
    deg_s = lax.dynamic_index_in_dim(deg, col * n_row + row, 0, False)
    deg_t = lax.dynamic_index_in_dim(deg, row * n_col + col, 0, False)
    rows = tile_rows.reshape(1, -1)
    cols = tile_cols.reshape(1, -1)
    masks = tile_masks.reshape(-1, 16, 128)
    hbm = spec(pl.ANY)
    n_rt, n_ct = 4 * n_col, 4 * n_row

    gathered, fwd_list, bwd_list = pl.pallas_call(
        functools.partial(gather_kernel, n_row),
        out_shape=(
            shaped((n_ct, 128, 128), BF16),
            shaped((8, SLOTS), I32),
            shaped((8, SLOTS), I32),
        ),
        in_specs=[spec()] * 4,
        out_specs=(hbm, spec(), spec()),
        scratch_shapes=[VMEM((4, 128, 128), BF16), dma(n_row), dma(n_row), pltpu.SemaphoreType.DMA],
        compiler_params=remote_params(0),
        name="gather_sources",
    )(features, deg_s, rows, cols)

    def product(kernel, codes, source, n_out, name):
        return pl.pallas_call(
            kernel,
            out_shape=shaped((n_out, 128, 128), BF16),
            in_specs=[spec(pltpu.SMEM), spec(), hbm],
            out_specs=spec(),
            scratch_shapes=[
                VMEM((776, 16, 128), I32),
                VMEM((n_out, 128, 128), F32),
                pltpu.SemaphoreType.DMA,
            ],
            compiler_params=pltpu.CompilerParams(vmem_limit_bytes=BIG),
            name=name,
        )(codes, source, masks)

    part = product(forward_kernel, fwd_list, gathered, n_rt, "tiles_forward")
    act, targets, gw = pl.pallas_call(
        functools.partial(layer_kernel, n_col, (512 * n_row * n_col) ** -0.5),
        out_shape=(
            shaped((512, 256), BF16),
            shaped((n_rt, 128, 128), BF16),
            shaped((128, 256), F32),
        ),
        in_specs=[hbm, spec(), spec(), spec()],
        out_specs=(spec(), hbm, spec()),
        scratch_shapes=[
            VMEM((n_col, 4, 128, 128), BF16),
            VMEM((4, 128, 128), BF16),
            dma(n_col),
            dma(n_col),
            dma(n_col),
            dma(n_col),
            pltpu.SemaphoreType.DMA,
            pltpu.SemaphoreType.DMA,
        ],
        compiler_params=remote_params(1),
        name="layer",
    )(part, weight, deg_t, cotangent)
    back = product(backward_kernel, bwd_list, targets, n_ct, "tiles_backward")
    grad_features, grad_weight = pl.pallas_call(
        functools.partial(finish_kernel, n_row, n_col),
        out_shape=(shaped((512, 128), F32), shaped((128, 256), F32)),
        in_specs=[hbm, spec(), spec()],
        out_specs=(spec(), spec()),
        scratch_shapes=[
            VMEM((n_row, 4, 128, 128), BF16),
            VMEM((n_row, 8, 256), F32),
            VMEM((8, 256), F32),
            VMEM((n_col, 8, 256), F32),
            VMEM((128, 256), F32),
            dma(n_row),
            dma(n_row),
            dma(n_row),
            dma(n_row),
            dma(n_col),
            dma(n_col),
            dma(n_row),
            dma(n_row),
            pltpu.SemaphoreType.DMA,
        ],
        compiler_params=remote_params(2),
        name="finish",
    )(back, deg_s, gw)
    return (act, grad_features, grad_weight)


def solution(mesh):
    in_specs = (
        P(("col", "row"), None),
        P(),
        P(),
        P("row", "col", None),
        P("row", "col", None),
        P("row", "col", None, None, None),
        P(("row", "col"), None),
    )
    out_specs = (P(("row", "col"), None), P(("col", "row"), None), P())
    return jax.shard_map(body, mesh=mesh, in_specs=in_specs, out_specs=out_specs, check_vma=False)
```

time: 944 us -> 162 us (0.17)
  waiting for transfers between devices: 376 us -> 0 us
  other arithmetic: 341 us -> 0 us
  Pallas kernels: 0 us -> 156 us
  matrix products: 118 us -> 0 us
  local copies, waits for them, and re-layouts: 91.6 us -> 5.05 us
  between operations: 13.9 us -> 0.71 us
    scatter-add x12 -> x0, other arithmetic: 337 us -> none  [the longest x6 235 us: backward_step(): return (totals.at[cols_here].add(contrib), None)]
    pallas_call x0 -> x5, Pallas kernels: none -> 156 us  [the longest x1 49.7 us: body(): pl.pallas_call(functools.partial(finish_kernel, n_row, n_col), out_shape=...]
    psum x1 -> x0, waiting for transfers between devices: 146 us -> none  [body(): grad_weight = lax.psum(grad_part, ('row', 'col'))]
    reduce_scatter x2 -> x0, waiting for transfers between devices: 140 us -> none  [the longest x1 73.5 us: body(): lax.psum_scatter(partial_value, 'col', scatter_dimension=0, tiled=True)]
    dot_general x15 -> x0, matrix products: 118 us -> none  [the longest x6 69.1 us: backward_step(): jnp.einsum('kji,kif->kjf', unpack_tiles(words_here), target_tiles[rows_he...]
    all_gather x2 -> x0, waiting for transfers between devices: 90.6 us -> none  [the longest x1 54.2 us: body(): gathered_rows = lax.all_gather(scaled_grad, 'col', axis=0, tiled=True)]
    gather x12 -> x0, local copies, waits for them, and re-layouts: 65.8 us -> none  [the longest x6 38 us: backward_step(): target_tiles[rows_here]]
    shift_right_arithmetic x36 -> x0, local copies, waits for them, and re-layouts: 16.6 us -> none  [unpack_tiles(): expanded = jnp.right_shift(mask_words[:, :, None, :], shifts[:, None]) & 1]
  transfers between devices with their start and end apart: 5 -> 0, of which waited for: 5 -> 0; matrix products, arithmetic and copies ran while one was open for 1% -> 0% of each run, Pallas kernels for 0% -> 0%
where the time goes in v1:
time: 162 us
  Pallas kernels  156 us (96%)
  local copies, waits for them, and re-layouts  5.05 us (3%)
    pallas_call x1, Pallas kernels, body(): pl.pallas_call(functools.partial(finish_kernel, n_row, n_col), out_shape=...  49.7 us
    pallas_call x2, Pallas kernels, product(): pl.pallas_call(kernel, out_shape=shaped((n_out, 128, 128), BF16), in_spec...  40.4 us
    pallas_call x1, Pallas kernels, body(): pl.pallas_call(functools.partial(gather_kernel, n_row), out_shape=(shaped...  34.1 us
    pallas_call x1, Pallas kernels, body(): pl.pallas_call(functools.partial(layer_kernel, n_col, (512 * n_row * n_co...  32.3 us
    unnamed x13, local copies, waits for them, and re-layouts  4.35 us

profile of v1, /device:TPU:1, one launch (start us, length us, event | category | flops | bytes accessed | tf_op | source)
XLA Modules:
  0.0 162.2 jit_solution(11499522360737279152)
XLA Ops:
  0.6 0.7 dynamic-slice_bitcast_fusion
  1.3 0.0 copy-start.1
  1.3 0.9 copy-done.1
  2.2 0.0 copy-start.3
  2.2 0.7 copy-done.3
  2.9 0.0 copy-start.4
  2.9 0.7 copy-done.4
  3.6 34.1 %gather_sources.1 = (bf16[64,128,128]{2,1,0:T(8,128)(2,1)S(1)}, s32[8,1024]{1,0:T(8,128)S(1)}, s32[8,1024]{1,0:T(8,128)S(1)}) custom-call(bf16[512,128]{1,0:T(8,128)(2,1)S(1)} %copy-done.1, s32[4,128]{1,0:T(4,128)S(1)} %get-tuple-element.20.deg, s32[1,768]{1,0:T(1,128)S(1)} %bitcast.8, s32[1,768]{1,0:T(1,128)S(1)} %bitcast.9), custom_call_target="tpu_custom_call" | custom-call | tf_op jit(solution)/shard_map/gather_sources/pallas_call | solution.py:354
  37.7 0.0 copy-start
  37.7 0.0 copy-start.2
  37.7 19.9 %tiles_forward.1.part = bf16[32,128,128]{2,1,0:T(8,128)(2,1)S(1)} custom-call(s32[8,1024]{1,0:T(8,128)S(1)} %get-tuple-element.11.codes, bf16[64,128,128]{2,1,0:T(8,128)(2,1)S(1)} %get-tuple-element.12.src, s32[768,16,128]{2,1,0:T(8,128)} %bitcast.10), custom_call_target="tpu_custom_call" | custom-call | tf_op jit(solution)/shard_map/tiles_forward/pallas_call | solution.py:369
  57.6 0.0 copy-done
  57.6 0.0 copy-done.2
  57.6 32.3 %layer.1 = (bf16[512,256]{1,0:T(8,128)(2,1)S(1)}, bf16[32,128,128]{2,1,0:T(8,128)(2,1)S(1)}, f32[128,256]{1,0:T(8,128)S(1)}) custom-call(bf16[32,128,128]{2,1,0:T(8,128)(2,1)S(1)} %tiles_forward.1.part, bf16[128,256]{1,0:T(8,128)(2,1)S(1)} %copy-done.2, s32[4,128]{1,0:T(4,128)S(1)} %get-tuple-element.19.deg, bf16[512,256]{1,0:T(8,128)(2,1)S(1)} %copy-done), custom_call_target="tpu_custom_call" | custom-call | tf_op jit(solution)/shard_map/layer/pallas_call | solution.py:384
  89.9 20.5 %tiles_backward.1.part = bf16[64,128,128]{2,1,0:T(8,128)(2,1)S(1)} custom-call(s32[8,1024]{1,0:T(8,128)S(1)} %get-tuple-element.14.codes, bf16[32,128,128]{2,1,0:T(8,128)(2,1)S(1)} %get-tuple-element.15.src, s32[768,16,128]{2,1,0:T(8,128)} %bitcast.11), custom_call_target="tpu_custom_call" | custom-call | tf_op jit(solution)/shard_map/tiles_backward/pallas_call | solution.py:369
  110.4 49.7 %finish.1 = (f32[512,128]{1,0:T(8,128)S(1)}, f32[128,256]{1,0:T(8,128)S(1)}) custom-call(bf16[64,128,128]{2,1,0:T(8,128)(2,1)S(1)} %tiles_backward.1.part, s32[4,128]{1,0:T(4,128)S(1)} %get-tuple-element.20.deg, f32[128,256]{1,0:T(8,128)S(1)} %get-tuple-element.16.gw), custom_call_target="tpu_custom_call" | custom-call | tf_op jit(solution)/shard_map/finish/pallas_call | solution.py:407
  160.1 0.7 copy.13
  160.8 0.7 copy.14
  161.5 0.7 copy.15
Async XLA Ops:
  1.3 0.9 copy-start.1
  2.2 0.7 copy-start.3
  2.9 0.7 copy-start.4
  37.7 19.9 %copy-start = (bf16[512,256]{1,0:T(8,128)(2,1)S(1)}, bf16[512,256]{1,0:T(8,128)(2,1)}, u32[]{:S(2)}) copy-start(bf16[512,256]{1,0:T(8,128)(2,1)} %cot.1) | copy-start | bytes 786436
  37.7 19.9 %copy-start.2 = (bf16[128,256]{1,0:T(8,128)(2,1)S(1)}, bf16[128,256]{1,0:T(8,128)(2,1)}, u32[]{:S(2)}) copy-start(bf16[128,256]{1,0:T(8,128)(2,1)} %weight.1) | copy-start | bytes 196612

commit v2 on v1

--- a/solution.py
+++ b/solution.py
@@ -34,13 +34,166 @@
     return hi, (x - hi.astype(F32)).astype(BF16)
 
 
-def greet(axis, count):
-    me = lax.axis_index(axis)
+class Place:
+    def __init__(self, axis):
+        self.axis = axis
+        me = lax.axis_index(axis)
+        if axis == "row":
+            self.core = lax.rem(me, 2)
+            chip = me // 2
+        else:
+            self.core = None
+            chip = me
+        self.p, self.q = chip // 4, lax.rem(chip, 4)
+
+    def chip(self, name):
+        p = 1 - self.p if name[0] == "x" else self.p
+        turn = {"": 0, "m": 3, "p": 1, "2": 2}[name[1:]]
+        return p * 4 + lax.rem(self.q + turn, 4)
+
+    def index(self, name):
+        chip = self.chip(name)
+        return chip if self.core is None else chip * 2 + self.core
+
+    def device(self, name):
+        if name == "twin":
+            return {self.axis: (self.p * 4 + self.q) * 2 + 1 - self.core}
+        return {self.axis: self.index(name)}
+
+    def partners(self):
+        return ["x", "om", "op"] + ([] if self.core is None else ["twin"])
+
+
+def send(src, dst, sems, i, device):
+    copy = pltpu.make_async_remote_copy(
+        src_ref=src,
+        dst_ref=dst,
+        send_sem=sems[0].at[i],
+        recv_sem=sems[1].at[i],
+        device_id=device,
+        device_id_type=MESH,
+    )
+    copy.start()
+    return copy
+
+
+def landed(ref, sem):
+    pltpu.make_async_copy(ref, ref, sem).wait()
+
+
+def greet(place):
     barrier = pltpu.get_barrier_semaphore()
-    for step in range(1, count):
-        peer = lax.rem(me + step, count)
-        pl.semaphore_signal(barrier, inc=1, device_id={axis: peer}, device_id_type=MESH)
-    pl.semaphore_wait(barrier, count - 1)
+    names = place.partners()
+    for name in names:
+        pl.semaphore_signal(
+            barrier, inc=1, device_id=place.device(name), device_id_type=MESH
+        )
+    pl.semaphore_wait(barrier, len(names))
+
+
+PIECES = [
+    ("x", 0, 4), ("om", 0, 4), ("op", 0, 4), ("o2", 0, 2), ("o2", 2, 2),
+    ("xm", 0, 4), ("xp", 0, 4), ("x2", 0, 2), ("x2", 2, 2), ("o", 0, 4),
+]
+
+
+def spread(place, mine, out, sems, twin_sems):
+    sent = []
+
+    def region(i):
+        name, first, tiles = PIECES[i]
+        return out.at[pl.ds(place.index(name) * 4 + first, tiles)]
+
+    def pass_on(i, to, dst, src):
+        sent.append(send(src, dst, sems, i, place.device(to)))
+
+    def twin(i, src):
+        if place.core is not None:
+            sent.append(send(src, region(i), twin_sems, i, place.device("twin")))
+
+    here = region(9)
+    for i, to in ((0, "x"), (1, "op"), (2, "om")):
+        pass_on(i, to, here, mine)
+    twin(9, mine)
+
+    def forward(i, targets):
+        ref = region(i)
+        landed(ref, sems[1].at[i])
+        for j, to in targets:
+            pass_on(j, to, ref, ref)
+        twin(i, ref)
+
+    def forward_half(i, j, to):
+        name, _, tiles = PIECES[i]
+        landed(region(i), sems[1].at[i])
+        half = out.at[pl.ds(place.index(name) * 4 + PIECES[j][1], 2)]
+        pass_on(j, to, half, half)
+        twin(i, region(i))
+
+    def finish():
+        forward(0, ((5, "op"), (6, "om")))
+        forward_half(1, 3, "op")
+        forward_half(2, 4, "om")
+        forward(3, ((7, "x"),))
+        forward(4, ((8, "x"),))
+        for i in (5, 6, 7, 8):
+            forward(i, ())
+        if place.core is not None:
+            for i in range(10):
+                name, first, tiles = PIECES[i]
+                index = place.chip(name) * 2 + 1 - place.core
+                landed(out.at[pl.ds(index * 4 + first, tiles)], twin_sems[1].at[i])
+        for copy in sent:
+            copy.wait_send()
+
+    return finish
+
+
+def gather_up(place, first, value, staged, got, sems):
+    sent = []
+
+    def go(i, src, dst, to):
+        sent.append(send(src, dst, sems, i, place.device(to)))
+
+    def stage(name, slot, tiles, *refs):
+        for t in tiles:
+            total = value(name, t)
+            for ref in refs:
+                total = total + ref[t].astype(F32)
+            staged[slot, t] = total.astype(BF16)
+
+    go(0, first("x2"), got.at[0], "x")
+    go(1, first("xm"), got.at[1], "om")
+    go(2, first("xp"), got.at[2], "op")
+    yield
+    landed(got.at[0], sems[1].at[0])
+    stage("o2", 3, range(4), got.at[0])
+    go(3, staged.at[3, pl.ds(0, 2)], got.at[3, pl.ds(0, 2)], "om")
+    go(4, staged.at[3, pl.ds(2, 2)], got.at[3, pl.ds(2, 2)], "op")
+    landed(got.at[1], sems[1].at[1])
+    landed(got.at[2], sems[1].at[2])
+    stage("x", 4, range(4), got.at[1], got.at[2])
+    go(5, staged.at[4], got.at[4], "x")
+    landed(got.at[3, pl.ds(0, 2)], sems[1].at[3])
+    stage("om", 5, (0, 1), got.at[3])
+    stage("om", 5, (2, 3))
+    go(6, staged.at[5], got.at[5], "om")
+    landed(got.at[3, pl.ds(2, 2)], sems[1].at[4])
+    stage("op", 6, (2, 3), got.at[3])
+    stage("op", 6, (0, 1))
+    go(7, staged.at[6], got.at[6], "op")
+    yield
+    for i in (4, 5, 6):
+        landed(got.at[i], sems[1].at[i + 1])
+    for copy in sent:
+        copy.wait_send()
+
+
+def gathered_tile(value, got, t):
+    total = value("o", t)
+    for i in (4, 5, 6):
+        total = total + got[i, t].astype(F32)
+    return total
 
 
 def order_list(keys, rows, cols, n_keys, group):
@@ -76,8 +229,10 @@
     return jnp.where(iota((8, SLOTS), 0) == 0, code, total)
 
 
-def gather_kernel(n, feat, deg, rows, cols, out, fwd_list, bwd_list, mine, send_sem, recv_sem, own_sem):
-    me = lax.axis_index("row")
+def gather_kernel(
+    feat, deg, rows, cols, out, fwd_list, bwd_list, mine, s1, r1, s2, r2, own_sem
+):
+    place = Place("row")
     lane = iota((128, 128), 1)
     perm = (iota((128, 128), 0) == ((lane & 15) * 8 + (lane >> 4))).astype(F32).astype(BF16)
     degrees = mm(deg[...].astype(F32).astype(BF16), perm)
@@ -91,29 +246,15 @@
             feat[t * 128 : (t + 1) * 128, :], perm, (((0,), (0,)), ((), ())), preferred_element_type=F32
         )
         mine[t] = (turned * inverse[t : t + 1, :] * shrink).astype(BF16)
-    greet("row", n)
-    copies = []
-    here = out.at[pl.ds(me * 4, 4)]
-    for step in range(1, n):
-        peer = lax.rem(me + step, n)
-        copy = pltpu.make_async_remote_copy(
-            src_ref=mine,
-            dst_ref=here,
-            send_sem=send_sem.at[step],
-            recv_sem=recv_sem.at[step],
-            device_id={"row": peer},
-            device_id_type=MESH,
-        )
-        copy.start()
-        copies.append(copy)
-    own = pltpu.make_async_copy(mine, here, own_sem)
+    greet(place)
+    finish = spread(place, mine, out, (s1, r1), (s2, r2))
+    own = pltpu.make_async_copy(mine, out.at[pl.ds(place.index("o") * 4, 4)], own_sem)
     own.start()
     r, c = rows[...], cols[...]
     fwd_list[...] = order_list(r, r, c, 1 << ROW_BITS, FWD_GROUP)
     bwd_list[...] = order_list(c, r, c, 1 << COL_BITS, BWD_GROUP)
     own.wait()
-    for copy in copies:
-        copy.wait()
+    finish()
 
 
 def unpack(words):
@@ -173,34 +314,27 @@
     out[...] = acc[...].astype(BF16)
 
 
-def layer_kernel(n, scale, part, weight, deg, cot, act, out, gw, got, mine, s1, r1, s2, r2, own1, own2):
-    me = lax.axis_index("col")
-    greet("col", n)
-    copies = []
-    for step in range(1, n):
-        peer = lax.rem(me + step, n)
-        copy = pltpu.make_async_remote_copy(
-            src_ref=part.at[pl.ds(peer * 4, 4)],
-            dst_ref=got.at[step],
-            send_sem=s1.at[step],
-            recv_sem=r1.at[step],
-            device_id={"col": peer},
-            device_id_type=MESH,
-        )
-        copy.start()
-        copies.append(copy)
-    own = pltpu.make_async_copy(part.at[pl.ds(me * 4, 4)], got.at[0], own1)
+def layer_kernel(
+    scale, part, weight, deg, cot, act, out, gw, held, staged, got, mine, s1, r1, s2, r2, own1, own2
+):
+    place = Place("col")
+    own = pltpu.make_async_copy(part, held, own1)
     own.start()
+    greet(place)
+
+    def value(name, t):
+        return held[place.chip(name), t].astype(F32)
+
+    steps = gather_up(place, lambda name: part.at[place.chip(name)], value, staged, got, (s1, r1))
+    next(steps)
     own.wait()
-    for copy in copies:
-        copy.wait()
+    for _ in steps:
+        pass
     w = weight[...]
     inverse = lax.rsqrt(deg[...].astype(F32))
     total = jnp.zeros((128, 256), F32)
     for t in range(4):
-        summed = got[0, t].astype(F32)
-        for step in range(1, n):
-            summed = summed + got[step, t].astype(F32)
+        summed = gathered_tile(value, got, t)
         factor = jnp.broadcast_to(inverse[t : t + 1, :], (128, 128))
         agg_t = summed * factor
         factor = factor.T
@@ -218,71 +352,75 @@
         mine[t] = lax.dot_general(
             scaled, w, (((1,), (1,)), ((), ())), preferred_element_type=F32
         ).astype(BF16)
-    here = out.at[pl.ds(me * 4, 4)]
-    copies = []
-    for step in range(1, n):
-        peer = lax.rem(me + step, n)
-        copy = pltpu.make_async_remote_copy(
-            src_ref=mine,
-            dst_ref=here,
-            send_sem=s2.at[step],
-            recv_sem=r2.at[step],
-            device_id={"col": peer},
-            device_id_type=MESH,
-        )
-        copy.start()
-        copies.append(copy)
-    own = pltpu.make_async_copy(mine, here, own2)
+    finish = spread(place, mine, out, (s2, r2), None)
+    own = pltpu.make_async_copy(mine, out.at[pl.ds(place.index("o") * 4, 4)], own2)
     own.start()
     gw[...] = total * scale
     own.wait()
-    for copy in copies:
-        copy.wait()
+    finish()
 
 
 def finish_kernel(
-    n_row, n_col, part, deg, gw, out, gw_out, got, gw_got, gw_row, gw_col, gw_all,
-    s1, r1, s2, r2, s3, r3, s4, r4, own_sem,
+    n_row, n_col, part, deg, gw, out, gw_out, held, from_twin, staged, got, gw_got, gw_row, gw_col, gw_all,
+    s0, r0, s1, r1, s2, r2, s3, r3, s4, r4, own_sem,
 ):
+    place = Place("row")
     row = lax.axis_index("row")
     col = lax.axis_index("col")
+    own = pltpu.make_async_copy(part.at[:, place.core], held, own_sem)
+    own.start()
     barrier = pltpu.get_barrier_semaphore()
+
+    def row_peer(step):
+        return {"row": lax.rem(row + step, n_row)}
+
+    def col_peer(step):
+        return {"col": lax.rem(col + step, n_col)}
+
     for step in range(1, n_row):
-        pl.semaphore_signal(
-            barrier, inc=1, device_id={"row": lax.rem(row + step, n_row)}, device_id_type=MESH
+        pl.semaphore_signal(barrier, inc=1, device_id=row_peer(step), device_id_type=MESH)
+    for step in range(1, n_col):
+        pl.semaphore_signal(barrier, inc=1, device_id=col_peer(step), device_id_type=MESH)
+    pl.semaphore_wait(barrier, n_row + n_col - 2)
+
+    order = ["x2", "xm", "xp", "o2", "x", "om", "op", "o"]
+    twins = [
+        send(
+            part.at[place.chip(name), 1 - place.core],
+            from_twin.at[k],
+            (s0, r0),
+            k,
+            place.device("twin"),
         )
-    for step in range(1, n_col):
-        pl.semaphore_signal(
-            barrier, inc=1, device_id={"col": lax.rem(col + step, n_col)}, device_id_type=MESH
+        for k, name in enumerate(order)
+    ]
+    weights = [
+        send(
+            gw.at[pl.ds(lax.rem(row + step, n_row) * 8, 8)],
+            gw_got.at[step],
+            (s2, r2),
+            step,
+            row_peer(step),
         )
-    pl.semaphore_wait(barrier, n_row + n_col - 2)
-
-    def send(src, dst, sems, step, axis, me, count):
-        copy = pltpu.make_async_remote_copy(
-            src_ref=src,
-            dst_ref=dst,
-            send_sem=sems[0].at[step],
-            recv_sem=sems[1].at[step],
-            device_id={axis: lax.rem(me + step, count)},
-            device_id_type=MESH,
-        )
-        copy.start()
-        return copy
-
-    weights = []
-    for step in range(1, n_row):
-        peer = lax.rem(row + step, n_row)
-        weights.append(
-            send(gw.at[pl.ds(peer * 8, 8)], gw_got.at[step], (s2, r2), step, "row", row, n_row)
-        )
-    main = []
-    for step in range(1, n_row):
-        peer = lax.rem(row + step, n_row)
-        main.append(
-            send(part.at[pl.ds(peer * 4, 4)], got.at[step], (s1, r1), step, "row", row, n_row)
-        )
-    own = pltpu.make_async_copy(part.at[pl.ds(row * 4, 4)], got.at[0], own_sem)
-    own.start()
+        for step in range(1, n_row)
+    ]
+    own.wait()
+
+    def value(name, t):
+        k = order.index(name)
+        return held[place.chip(name), t].astype(F32) + from_twin[k, t].astype(F32)
+
+    def first(name):
+        k = order.index(name)
+        landed(from_twin.at[k], r0.at[k])
+        for t in range(4):
+            staged[k, t] = value(name, t).astype(BF16)
+        return staged.at[k]
+
+    steps = gather_up(place, first, value, staged, got, (s1, r1))
+    next(steps)
+    for k in range(3, 8):
+        landed(from_twin.at[k], r0.at[k])
     for copy in weights:
         copy.wait()
     summed = gw[pl.ds(row * 8, 8), :]
@@ -291,29 +429,35 @@
     gw_row[...] = summed
     gw_col[pl.ds(col, 1)] = summed[None]
     weights = [
-        send(gw_row, gw_col.at[col], (s3, r3), step, "col", col, n_col) for step in range(1, n_col)
+        send(gw_row, gw_col.at[col], (s3, r3), step, col_peer(step)) for step in range(1, n_col)
     ]
+    next(steps)
     for copy in weights:
-        copy.wait()
+        copy.wait_send()
+    for step in range(1, n_col):
+        landed(gw_col.at[lax.rem(col + n_col - step, n_col)], r3.at[step])
     summed = gw_col[0]
     for c in range(1, n_col):
         summed = summed + gw_col[c]
     mine = gw_all.at[pl.ds(row * 8, 8)]
     gw_all[pl.ds(row * 8, 8), :] = summed
-    weights = [send(mine, mine, (s4, r4), step, "row", row, n_row) for step in range(1, n_row)]
+    weights = [send(mine, mine, (s4, r4), step, row_peer(step)) for step in range(1, n_row)]
     inverse = lax.rsqrt(deg[...].astype(F32))
-    own.wait()
-    for copy in main:
-        copy.wait()
+    for _ in steps:
+        pass
+    lane_b = iota((128, 128), 0) >> 4
+    grow = jnp.zeros((128, 128), F32)
+    for b in range(8):
+        grow = jnp.where(lane_b == b, 2.0**-b, grow)
     for t in range(4):
         factor = jnp.broadcast_to(inverse[t : t + 1, :], (128, 128)).T
+        total = gathered_tile(value, got, t) * grow
         for b in range(8):
-            total = got[0, t, b * 16 : (b + 1) * 16, :].astype(F32)
-            for step in range(1, n_row):
-                total = total + got[step, t, b * 16 : (b + 1) * 16, :].astype(F32)
-            out[pl.ds(t * 128 + b, 16, stride=8), :] = total * (2.0**-b)
+            out[pl.ds(t * 128 + b, 16, stride=8), :] = total[b * 16 : (b + 1) * 16, :]
         rows = pl.ds(t * 128, 128)
         out[rows, :] = out[rows, :] * factor
+    for copy in twins:
+        copy.wait_send()
     for copy in weights:
         copy.wait()
     gw_out[...] = gw_all[...]
@@ -352,7 +496,7 @@
     n_rt, n_ct = 4 * n_col, 4 * n_row
 
     gathered, fwd_list, bwd_list = pl.pallas_call(
-        functools.partial(gather_kernel, n_row),
+        gather_kernel,
         out_shape=(
             shaped((n_ct, 128, 128), BF16),
             shaped((8, SLOTS), I32),
@@ -360,7 +504,7 @@
         ),
         in_specs=[spec()] * 4,
         out_specs=(hbm, spec(), spec()),
-        scratch_shapes=[VMEM((4, 128, 128), BF16), dma(n_row), dma(n_row), pltpu.SemaphoreType.DMA],
+        scratch_shapes=[VMEM((4, 128, 128), BF16), dma(10), dma(10), dma(10), dma(10), pltpu.SemaphoreType.DMA],
         compiler_params=remote_params(0),
         name="gather_sources",
     )(features, deg_s, rows, cols)
@@ -382,7 +526,7 @@
 
     part = product(forward_kernel, fwd_list, gathered, n_rt, "tiles_forward")
     act, targets, gw = pl.pallas_call(
-        functools.partial(layer_kernel, n_col, (512 * n_row * n_col) ** -0.5),
+        functools.partial(layer_kernel, (512 * n_row * n_col) ** -0.5),
         out_shape=(
             shaped((512, 256), BF16),
             shaped((n_rt, 128, 128), BF16),
@@ -391,18 +535,20 @@
         in_specs=[hbm, spec(), spec(), spec()],
         out_specs=(spec(), hbm, spec()),
         scratch_shapes=[
-            VMEM((n_col, 4, 128, 128), BF16),
+            VMEM((8, 4, 128, 128), BF16),
+            VMEM((8, 4, 128, 128), BF16),
+            VMEM((7, 4, 128, 128), BF16),
             VMEM((4, 128, 128), BF16),
-            dma(n_col),
-            dma(n_col),
-            dma(n_col),
-            dma(n_col),
+            dma(8),
+            dma(8),
+            dma(10),
+            dma(10),
             pltpu.SemaphoreType.DMA,
             pltpu.SemaphoreType.DMA,
         ],
         compiler_params=remote_params(1),
         name="layer",
-    )(part, weight, deg_t, cotangent)
+    )(part.reshape(8, 4, 128, 128), weight, deg_t, cotangent)
     back = product(backward_kernel, bwd_list, targets, n_ct, "tiles_backward")
     grad_features, grad_weight = pl.pallas_call(
         functools.partial(finish_kernel, n_row, n_col),
@@ -410,13 +556,18 @@
         in_specs=[hbm, spec(), spec()],
         out_specs=(spec(), spec()),
         scratch_shapes=[
-            VMEM((n_row, 4, 128, 128), BF16),
+            VMEM((8, 4, 128, 128), BF16),
+            VMEM((8, 4, 128, 128), BF16),
+            VMEM((8, 4, 128, 128), BF16),
+            VMEM((7, 4, 128, 128), BF16),
             VMEM((n_row, 8, 256), F32),
             VMEM((8, 256), F32),
             VMEM((n_col, 8, 256), F32),
             VMEM((128, 256), F32),
-            dma(n_row),
-            dma(n_row),
+            dma(8),
+            dma(8),
+            dma(8),
+            dma(8),
             dma(n_row),
             dma(n_row),
             dma(n_col),
@@ -427,7 +578,7 @@
         ],
         compiler_params=remote_params(2),
         name="finish",
-    )(back, deg_s, gw)
+    )(back.reshape(8, 2, 4, 128, 128), deg_s, gw)
     return (act, grad_features, grad_weight)
 
 

time: 162 us -> 121 us (0.75)
  Pallas kernels: 156 us -> 115 us
    pallas_call x1, Pallas kernels: 49.7 us -> 24.3 us  [body(): pl.pallas_call(functools.partial(finish_kernel, n_row, n_col), out_shape=...]
    pallas_call x2, Pallas kernels: 66.4 us -> 49.4 us  [the longest x1 29.9 us: body(): pl.pallas_call(functools.partial(layer_kernel, (512 * n_row * n_col) ** (...]
where the time goes in v2:
time: 121 us
  Pallas kernels  115 us (95%)
  local copies, waits for them, and re-layouts  5.05 us (4%)
    pallas_call x2, Pallas kernels, product(): pl.pallas_call(kernel, out_shape=shaped((n_out, 128, 128), BF16), in_spec...  41.1 us
    pallas_call x1, Pallas kernels, body(): pl.pallas_call(functools.partial(layer_kernel, (512 * n_row * n_col) ** (...  29.9 us
    pallas_call x1, Pallas kernels, body(): pl.pallas_call(functools.partial(finish_kernel, n_row, n_col), out_shape=...  24.3 us
    pallas_call x1, Pallas kernels, body(): pl.pallas_call(gather_kernel, out_shape=(shaped((n_ct, 128, 128), BF16),...  19.6 us
    unnamed x13, local copies, waits for them, and re-layouts  4.35 us

profile of v2, /device:TPU:1, one launch (start us, length us, event | category | flops | bytes accessed | tf_op | source)
XLA Modules:
  0.0 120.6 jit_solution(5506520569650304220)
XLA Ops:
  0.6 0.7 dynamic-slice_bitcast_fusion
  1.3 0.0 copy-start.1
  1.3 0.9 copy-done.1
  2.2 0.0 copy-start.3
  2.2 0.7 copy-done.3
  2.9 0.0 copy-start.4
  2.9 0.7 copy-done.4
  3.6 19.6 %gather_sources.1 = (bf16[64,128,128]{2,1,0:T(8,128)(2,1)S(1)}, s32[8,1024]{1,0:T(8,128)S(1)}, s32[8,1024]{1,0:T(8,128)S(1)}) custom-call(bf16[512,128]{1,0:T(8,128)(2,1)S(1)} %copy-done.1, s32[4,128]{1,0:T(4,128)S(1)} %get-tuple-element.20.deg, s32[1,768]{1,0:T(1,128)S(1)} %bitcast.12, s32[1,768]{1,0:T(1,128)S(1)} %bitcast.13), custom_call_target="tpu_custom_call" | custom-call | tf_op jit(solution)/shard_map/gather_sources/pallas_call | solution.py:498
  23.2 0.0 copy-start
  23.2 0.0 copy-start.2
  23.2 20.2 %tiles_forward.1 = bf16[32,128,128]{2,1,0:T(8,128)(2,1)S(1)} custom-call(s32[8,1024]{1,0:T(8,128)S(1)} %get-tuple-element.11.codes, bf16[64,128,128]{2,1,0:T(8,128)(2,1)S(1)} %get-tuple-element.12.src, s32[768,16,128]{2,1,0:T(8,128)} %bitcast.14), custom_call_target="tpu_custom_call" | custom-call | tf_op jit(solution)/shard_map/tiles_forward/pallas_call | solution.py:513
  43.4 0.0 copy-done
  43.4 0.0 copy-done.2
  43.4 29.9 %layer.1 = (bf16[512,256]{1,0:T(8,128)(2,1)S(1)}, bf16[32,128,128]{2,1,0:T(8,128)(2,1)S(1)}, f32[128,256]{1,0:T(8,128)S(1)}) custom-call(bf16[8,4,128,128]{3,2,1,0:T(8,128)(2,1)S(1)} %bitcast.11, bf16[128,256]{1,0:T(8,128)(2,1)S(1)} %copy-done.2, s32[4,128]{1,0:T(4,128)S(1)} %get-tuple-element.19.deg, bf16[512,256]{1,0:T(8,128)(2,1)S(1)} %copy-done), custom_call_target="tpu_custom_call" | custom-call | tf_op jit(solution)/shard_map/layer/pallas_call | solution.py:528
  73.3 20.9 %tiles_backward.1 = bf16[64,128,128]{2,1,0:T(8,128)(2,1)S(1)} custom-call(s32[8,1024]{1,0:T(8,128)S(1)} %get-tuple-element.14.codes, bf16[32,128,128]{2,1,0:T(8,128)(2,1)S(1)} %get-tuple-element.15.src, s32[768,16,128]{2,1,0:T(8,128)} %bitcast.15), custom_call_target="tpu_custom_call" | custom-call | tf_op jit(solution)/shard_map/tiles_backward/pallas_call | solution.py:513
  94.2 24.3 %finish.1 = (f32[512,128]{1,0:T(8,128)S(1)}, f32[128,256]{1,0:T(8,128)S(1)}) custom-call(bf16[8,2,4,128,128]{4,3,2,1,0:T(8,128)(2,1)S(1)} %bitcast.10, s32[4,128]{1,0:T(4,128)S(1)} %get-tuple-element.20.deg, f32[128,256]{1,0:T(8,128)S(1)} %get-tuple-element.16.gw), custom_call_target="tpu_custom_call" | custom-call | tf_op jit(solution)/shard_map/finish/pallas_call | solution.py:553
  118.6 0.7 copy.13
  119.3 0.7 copy.14
  120.0 0.7 copy.15
Async XLA Ops:
  1.3 0.9 copy-start.1
  2.2 0.7 copy-start.3
  2.9 0.7 copy-start.4
  23.2 20.2 %copy-start = (bf16[512,256]{1,0:T(8,128)(2,1)S(1)}, bf16[512,256]{1,0:T(8,128)(2,1)}, u32[]{:S(2)}) copy-start(bf16[512,256]{1,0:T(8,128)(2,1)} %cot.1) | copy-start | bytes 786436
  23.2 20.2 %copy-start.2 = (bf16[128,256]{1,0:T(8,128)(2,1)S(1)}, bf16[128,256]{1,0:T(8,128)(2,1)}, u32[]{:S(2)}) copy-start(bf16[128,256]{1,0:T(8,128)(2,1)} %weight.1) | copy-start | bytes 196612

commit v3 on v2

v3 whole, which is shorter than its diff:
```python
import functools
import itertools

import jax
import jax.numpy as jnp
from jax import lax
from jax.experimental import pallas as pl
from jax.experimental.pallas import tpu as pltpu
from jax.sharding import PartitionSpec as P

F32 = jnp.float32
BF16 = jnp.bfloat16
I32 = jnp.int32
MESH = pl.DeviceIdType.MESH
VMEM = pltpu.VMEM
SLOTS = 1024
ROW_BITS = 5
COL_BITS = 6
CODE_BITS = ROW_BITS + COL_BITS
FRESH = 24
GROUP, UNROLL = 4, 16
FWD_ROUNDS, BWD_ROUNDS = 14, 15
EMPTY = BWD_ROUNDS * UNROLL
BIG = 56 * 1024 * 1024


def mm(a, b):
    return jnp.dot(a, b, preferred_element_type=F32)


def iota(shape, dim):
    return lax.broadcasted_iota(I32, shape, dim)


def split(x):
    hi = x.astype(BF16)
    return hi, (x - hi.astype(F32)).astype(BF16)


class Place:
    def __init__(self, axis):
        self.axis = axis
        me = lax.axis_index(axis)
        if axis == "row":
            self.core = lax.rem(me, 2)
            chip = me // 2
        else:
            self.core = None
            chip = me
        self.p, self.q = chip // 4, lax.rem(chip, 4)

    def chip(self, name):
        p = 1 - self.p if name[0] == "x" else self.p
        turn = {"": 0, "m": 3, "p": 1, "2": 2}[name[1:]]
        return p * 4 + lax.rem(self.q + turn, 4)

    def index(self, name):
        chip = self.chip(name)
        return chip if self.core is None else chip * 2 + self.core

    def device(self, name):
        if name == "twin":
            return {self.axis: (self.p * 4 + self.q) * 2 + 1 - self.core}
        return {self.axis: self.index(name)}

    def partners(self):
        return ["x", "om", "op"] + ([] if self.core is None else ["twin"])


def send(src, dst, sems, i, device):
    copy = pltpu.make_async_remote_copy(
        src_ref=src,
        dst_ref=dst,
        send_sem=sems[0].at[i],
        recv_sem=sems[1].at[i],
        device_id=device,
        device_id_type=MESH,
    )
    copy.start()
    return copy


def landed(ref, sem):
    pltpu.make_async_copy(ref, ref, sem).wait()


class Place:
    def __init__(self, axis):
        self.axis = axis
        me = lax.axis_index(axis)
        if axis == "row":
            self.core = lax.rem(me, 2)
            chip = me // 2
        else:
            self.core = None
            chip = me
        self.p, self.q = chip // 4, lax.rem(chip, 4)

    def chip(self, name):
        p = 1 - self.p if name[0] == "x" else self.p
        turn = {"": 0, "m": 3, "p": 1, "2": 2}[name[1:]]
        return p * 4 + lax.rem(self.q + turn, 4)

    def index(self, name):
        chip = self.chip(name)
        return chip if self.core is None else chip * 2 + self.core

    def device(self, name):
        if name == "twin":
            return {self.axis: (self.p * 4 + self.q) * 2 + 1 - self.core}
        return {self.axis: self.index(name)}

def send(src, dst, sems, i, device):
    copy = pltpu.make_async_remote_copy(
        src_ref=src,
        dst_ref=dst,
        send_sem=sems[0].at[i],
        recv_sem=sems[1].at[i],
        device_id=device,
        device_id_type=MESH,
    )
    copy.start()
    return copy


def landed(ref, sem):
    pltpu.make_async_copy(ref, ref, sem).wait()


def together(*parts):
    for _ in itertools.zip_longest(*parts):
        pass


PIECES = [
    ("x", 0, 2), ("om", 0, 2), ("op", 0, 2), ("o2", 0, 1), ("o2", 1, 1),
    ("xm", 0, 2), ("xp", 0, 2), ("x2", 0, 1), ("x2", 1, 1), ("o", 0, 2),
]


def spread(place, mine, out, sems, twin_sems, chunk, sent):
    low = 10 * chunk

    def part(index, first, tiles):
        return out.at[pl.ds(index * 4 + 2 * chunk + first, tiles)]

    def region(i):
        name, first, tiles = PIECES[i]
        return part(place.index(name), first, tiles)

    def pass_on(i, to, dst, src):
        sent.append(send(src, dst, sems, low + i, place.device(to)))

    def twin(i, src):
        if place.core is not None:
            sent.append(send(src, region(i), twin_sems, low + i, place.device("twin")))

    own = mine.at[pl.ds(2 * chunk, 2)]
    for i, to in ((0, "x"), (1, "op"), (2, "om")):
        pass_on(i, to, region(9), own)
    twin(9, own)
    yield

    def forward(i, targets):
        ref = region(i)
        landed(ref, sems[1].at[low + i])
        for j, to in targets:
            pass_on(j, to, ref, ref)
        twin(i, ref)

    def forward_half(i, j, to):
        landed(region(i), sems[1].at[low + i])
        half = part(place.index(PIECES[i][0]), PIECES[j][1], 1)
        pass_on(j, to, half, half)
        twin(i, region(i))

    forward(0, ((5, "op"), (6, "om")))
    yield
    forward_half(1, 3, "op")
    yield
    forward_half(2, 4, "om")
    yield
    forward(3, ((7, "x"),))
    yield
    forward(4, ((8, "x"),))
    yield
    for i in (5, 6, 7, 8):
        forward(i, ())
        yield
    if place.core is not None:
        for i in range(10):
            name, first, tiles = PIECES[i]
            ref = part(place.chip(name) * 2 + 1 - place.core, first, tiles)
            landed(ref, twin_sems[1].at[low + i])


def gather_up(place, ready, value, staged, got, sems, chunk, sent):
    low = 8 * chunk
    t0, t1 = 2 * chunk, 2 * chunk + 1
    both = pl.ds(t0, 2)

    def go(i, slot, into, at, to):
        src, dst = staged.at[slot, at], got.at[into, at]
        sent.append(send(src, dst, sems, low + i, place.device(to)))

    def wait(i, into, at=both):
        landed(got.at[into, at], sems[1].at[low + i])

    def stage(name, slot, tiles, *slots):
        for t in tiles:
            total = value(name, t)
            for k in slots:
                total = total + got[k, t].astype(F32)
            staged[slot, t] = total.astype(BF16)

    for i, name, to in ((0, "x2", "x"), (1, "xm", "om"), (2, "xp", "op")):
        ready(name)
        stage(name, i, (t0, t1))
        go(i, i, i, both, to)
    yield
    wait(0, 0)
    ready("o2")
    stage("o2", 3, (t0, t1), 0)
    go(3, 3, 3, pl.ds(t0, 1), "om")
    go(4, 3, 3, pl.ds(t1, 1), "op")
    yield
    wait(1, 1)
    wait(2, 2)
    ready("x")
    stage("x", 4, (t0, t1), 1, 2)
    go(5, 4, 4, both, "x")
    yield
    ready("om")
    wait(3, 3, pl.ds(t0, 1))
    stage("om", 5, (t0,), 3)
    stage("om", 5, (t1,))
    go(6, 5, 5, both, "om")
    yield
    ready("op")
    wait(4, 3, pl.ds(t1, 1))
    stage("op", 6, (t1,), 3)
    stage("op", 6, (t0,))
    go(7, 6, 6, both, "op")
    yield
    ready("o")
    for i in (4, 5, 6):
        wait(i + 1, i)
    yield


def gathered_tile(value, got, t):
    total = value("o", t)
    for i in (4, 5, 6):
        total = total + got[i, t].astype(F32)
    return total


def order_list(keys, rows, cols, n_keys, group):
    cap = keys.shape[1]
    hot = iota((n_keys, cap), 0) == keys
    hot_f = hot.astype(F32)
    upper = (iota((cap, cap), 0) < iota((cap, cap), 1)).astype(F32).astype(BF16)
    rank = mm(hot_f.astype(BF16), upper)
    count = jnp.sum(hot_f, axis=1, keepdims=True)
    groups = jnp.floor((count + (group - 1)) * (1.0 / group))
    wide = jnp.broadcast_to(groups, (n_keys, 128)).astype(BF16)
    lower = (iota((n_keys, n_keys), 1) < iota((n_keys, n_keys), 0)).astype(F32).astype(BF16)
    base = mm(lower, wide)[:, :1] * group
    pos = jnp.sum(hot_f * (rank + base), axis=0, keepdims=True)
    opens = jnp.sum(hot_f * rank, axis=0, keepdims=True) < 0.5
    place = (iota((SLOTS, cap), 0) == pos.astype(I32)).astype(F32).astype(BF16)
    which = iota((8, cap), 0)
    slot = iota((8, cap), 1)
    vals = jnp.where(
        which == 0,
        slot >> 4,
        jnp.where(
            which == 1,
            slot & 15,
            jnp.where(which == 2, cols, jnp.where(which == 3, rows, jnp.where(which == 4, 1, opens.astype(I32)))),
        ),
    )
    vals = vals.astype(F32).astype(BF16)
    found = lax.dot_general(vals, place, (((1,), (1,)), ((), ())), preferred_element_type=F32)
    f = found.astype(I32)
    code = ((f[0:1] * 16 + f[1:2]) << CODE_BITS) | (f[2:3] << ROW_BITS) | f[3:4]
    code = jnp.where(f[4:5] > 0, code, cap << CODE_BITS)
    code = code | (f[5:6] << FRESH)
    last = jnp.where(groups > 0.5, base * (1.0 / group) + groups - 1.0, 1.0 * EMPTY)
    square = (n_keys, SLOTS)
    last = jnp.sum(jnp.where(iota(square, 0) == iota(square, 1), last, 0.0), axis=0, keepdims=True)
    return jnp.where(iota((8, SLOTS), 0) == 0, code, last.astype(I32))


def gather_kernel(
    feat, deg, rows, cols, out, fwd_list, bwd_list, mine, s1, r1, s2, r2, own_sem
):
    place = Place("row")
    lane = iota((128, 128), 1)
    perm = (iota((128, 128), 0) == ((lane & 15) * 8 + (lane >> 4))).astype(F32).astype(BF16)
    degrees = mm(deg[...].astype(F32).astype(BF16), perm)
    bucket = iota((1, 128), 1) >> 4
    shrink = jnp.zeros((1, 128), F32)
    for b in range(8):
        shrink = jnp.where(bucket == b, 2.0**-b, shrink)
    inverse = lax.rsqrt(degrees)
    for t in range(4):
        turned = lax.dot_general(
            feat[t * 128 : (t + 1) * 128, :], perm, (((0,), (0,)), ((), ())), preferred_element_type=F32
        )
        mine[t] = (turned * inverse[t : t + 1, :] * shrink).astype(BF16)
    barrier = pltpu.get_barrier_semaphore()
    partners = ["x", "om", "op", "twin"]
    for name in partners:
        pl.semaphore_signal(barrier, inc=1, device_id=place.device(name), device_id_type=MESH)
    pl.semaphore_wait(barrier, len(partners))
    sent = []
    chunks = [spread(place, mine, out, (s1, r1), (s2, r2), c, sent) for c in range(2)]
    for chunk in chunks:
        next(chunk)
    own = pltpu.make_async_copy(mine, out.at[pl.ds(place.index("o") * 4, 4)], own_sem)
    own.start()
    r, c = rows[...], cols[...]
    fwd_list[...] = order_list(r, r, c, 1 << ROW_BITS, GROUP)
    bwd_list[...] = order_list(c, r, c, 1 << COL_BITS, GROUP)
    own.wait()
    together(*chunks)
    for copy in sent:
        copy.wait_send()


def unpack(held, codes):
    words = jnp.concatenate([held[pl.ds((k >> CODE_BITS) & 1023, 1)] for k in codes], axis=0)
    parts = [(words & (1 << b)).astype(F32).astype(BF16) for b in range(8)]
    return jnp.concatenate(parts, axis=1)


def run_tiles(rounds, codes, product, acc, run):
    acc[...] = jnp.zeros_like(acc)

    def body(i, carry):
        total = acc[...]
        for u in range(UNROLL):
            at = (i * UNROLL + u) * GROUP
            code = [codes[0, at + g] for g in range(GROUP)]
            keep = (1 - ((code[0] >> FRESH) & 1)).astype(F32)
            total = total * keep + product(code)
            run[i * UNROLL + u] = total
        acc[...] = total
        return carry

    lax.fori_loop(0, rounds, body, 0)


def main_kernel(
    scale, n_row, n_col, fwd, bwd, src, masks, weight, deg_t, deg_s, cot, act, out, gw_out,
    held, acc, run, targets, mine, staged_c, got_c, twin_out, from_twin, staged_r, got_r,
    gw, gw_got, gw_row, gw_col, gw_all,
    sc, rc, sg, rg, s0, r0, sr, rr, s2, r2, s3, r3, s4, r4, mask_sem, own_sem,
):
    row = lax.axis_index("row")
    col = lax.axis_index("col")
    rows_place, cols_place = Place("row"), Place("col")
    load = pltpu.make_async_copy(masks, held.at[pl.ds(0, 768)], mask_sem)
    load.start()
    barrier = pltpu.get_barrier_semaphore()

    def row_peer(step):
        return {"row": lax.rem(row + step, n_row)}

    def col_peer(step):
        return {"col": lax.rem(col + step, n_col)}

    for step in range(1, n_row):
        pl.semaphore_signal(barrier, inc=1, device_id=row_peer(step), device_id_type=MESH)
    for step in range(1, n_col):
        pl.semaphore_signal(barrier, inc=1, device_id=col_peer(step), device_id_type=MESH)
    held[768] = jnp.zeros((16, 128), I32)
    run[EMPTY] = jnp.zeros((128, 128), F32)
    load.wait()

    def forward(code):
        lhs = jnp.concatenate(
            [src[(k >> ROW_BITS) & ((1 << COL_BITS) - 1)] for k in code], axis=1
        )
        return mm(lhs, unpack(held, code).reshape(GROUP * 128, 128))

    run_tiles(FWD_ROUNDS, fwd, forward, acc, run)
    pl.semaphore_wait(barrier, n_row + n_col - 2)
    sent = []

    def forward_sum(name, t):
        return run[fwd[1, cols_place.index(name) * 4 + t]]

    ups = [
        gather_up(cols_place, lambda name: None, forward_sum, staged_c, got_c, (sc, rc), c, sent)
        for c in range(2)
    ]
    for _ in range(5):
        for up in ups:
            next(up)
    w = weight[...]
    inverse = lax.rsqrt(deg_t[...].astype(F32))
    total = jnp.zeros((128, 256), F32)
    downs = []
    for c in range(2):
        next(ups[c])
        for t in (2 * c, 2 * c + 1):
            summed = gathered_tile(forward_sum, got_c, t)
            factor = jnp.broadcast_to(inverse[t : t + 1, :], (128, 128))
            agg_t = summed * factor
            factor = factor.T
            factor = jnp.concatenate([factor, factor], axis=1)
            t_hi, t_lo = split(agg_t)
            hi, lo = split(agg_t.T)
            pre = mm(hi, w) + mm(lo, w)
            slope = jnp.where(pre > 0, 1.0, jnp.exp(jnp.minimum(pre, 0.0)))
            rows = pl.ds(t * 128, 128)
            act[rows, :] = jnp.where(pre > 0, pre, slope - 1.0).astype(BF16)
            grad = cot[rows, :].astype(F32) * slope
            g_hi, g_lo = split(grad)
            total = total + (mm(t_hi, g_hi) + (mm(t_lo, g_hi) + mm(t_hi, g_lo)))
            scaled = (grad * factor).astype(BF16)
            mine[t] = lax.dot_general(
                scaled, w, (((1,), (1,)), ((), ())), preferred_element_type=F32
            ).astype(BF16)
        down = spread(cols_place, mine, targets, (sg, rg), None, c, sent)
        next(down)
        downs.append(down)
    own = pltpu.make_async_copy(mine, targets.at[pl.ds(col * 4, 4)], own_sem)
    own.start()
    gw[...] = total * scale
    weights = [
        send(
            gw.at[pl.ds(lax.rem(row + step, n_row) * 8, 8)],
            gw_got.at[step],
            (s2, r2),
            step,
            row_peer(step),
        )
        for step in range(1, n_row)
    ]
    own.wait()
    together(*downs)

    def backward(code):
        rhs = jnp.concatenate([targets[k & ((1 << ROW_BITS) - 1)] for k in code], axis=0)
        tiles = unpack(held, code)
        return mm(jnp.concatenate([tiles[g] for g in range(GROUP)], axis=1), rhs)

    run_tiles(BWD_ROUNDS, bwd, backward, acc, run)

    order = ["x2", "xm", "xp", "o2", "x", "om", "op", "o"]
    for k, name in enumerate(order):
        index = rows_place.chip(name) * 2 + 1 - rows_place.core
        for t in range(4):
            twin_out[k, t] = run[bwd[1, index * 4 + t]].astype(BF16)
        sent.append(
            send(twin_out.at[k], from_twin.at[k], (s0, r0), k, rows_place.device("twin"))
        )
    for copy in weights:
        copy.wait()
    summed = gw[pl.ds(row * 8, 8), :]
    for step in range(1, n_row):
        summed = summed + gw_got[step]
    gw_row[...] = summed
    gw_col[pl.ds(col, 1)] = summed[None]
    for step in range(1, n_col):
        sent.append(send(gw_row, gw_col.at[col], (s3, r3), step, col_peer(step)))

    arrived = set()

    def ready(name):
        if name not in arrived:
            k = order.index(name)
            landed(from_twin.at[k], r0.at[k])
            arrived.add(name)

    def backward_sum(name, t):
        mine_sum = run[bwd[1, rows_place.index(name) * 4 + t]]
        return mine_sum + from_twin[order.index(name), t].astype(F32)

    ups = [
        gather_up(rows_place, ready, backward_sum, staged_r, got_r, (sr, rr), c, sent)
        for c in range(2)
    ]
    for _ in range(4):
        for up in ups:
            next(up)
    for step in range(1, n_col):
        landed(gw_col.at[lax.rem(col + n_col - step, n_col)], r3.at[step])
    summed = gw_col[0]
    for c in range(1, n_col):
        summed = summed + gw_col[c]
    gw_mine = gw_all.at[pl.ds(row * 8, 8)]
    gw_all[pl.ds(row * 8, 8), :] = summed
    weights = [send(gw_mine, gw_mine, (s4, r4), step, row_peer(step)) for step in range(1, n_row)]
    inverse = lax.rsqrt(deg_s[...].astype(F32))
    for up in ups:
        next(up)
    bucket = iota((128, 128), 0) >> 4
    grow = jnp.zeros((128, 128), F32)
    for b in range(8):
        grow = jnp.where(bucket == b, 2.0**-b, grow)
    for c in range(2):
        next(ups[c])
        for t in (2 * c, 2 * c + 1):
            factor = jnp.broadcast_to(inverse[t : t + 1, :], (128, 128)).T
            summed = gathered_tile(backward_sum, got_r, t) * grow
            for b in range(8):
                out[pl.ds(t * 128 + b, 16, stride=8), :] = summed[b * 16 : (b + 1) * 16, :]
            rows = pl.ds(t * 128, 128)
            out[rows, :] = out[rows, :] * factor
    for copy in sent:
        copy.wait_send()
    for copy in weights:
        copy.wait_send()
    for step in range(1, n_row):
        peer = lax.rem(row + n_row - step, n_row)
        landed(gw_all.at[pl.ds(peer * 8, 8)], r4.at[step])
    gw_out[...] = gw_all[...]


def spec(space=VMEM):
    return pl.BlockSpec(memory_space=space)


def shaped(shape, dtype):
    return jax.ShapeDtypeStruct(shape, dtype)


def remote_params(number):
    return pltpu.CompilerParams(
        collective_id=number, has_side_effects=True, vmem_limit_bytes=BIG
    )


def dma(count):
    return pltpu.SemaphoreType.DMA((count,))


def body(features, weight, degrees, tile_rows, tile_cols, tile_masks, cotangent):
    row = lax.axis_index("row")
    col = lax.axis_index("col")
    n_row = lax.axis_size("row")
    n_col = lax.axis_size("col")
    deg = degrees.reshape(n_row * n_col, 4, 128)
    deg_s = lax.dynamic_index_in_dim(deg, col * n_row + row, 0, False)
    deg_t = lax.dynamic_index_in_dim(deg, row * n_col + col, 0, False)
    rows = tile_rows.reshape(1, -1)
    cols = tile_cols.reshape(1, -1)
    masks = tile_masks.reshape(-1, 16, 128)
    hbm = spec(pl.ANY)
    n_rt, n_ct = 4 * n_col, 4 * n_row

    gathered, fwd_list, bwd_list = pl.pallas_call(
        gather_kernel,
        out_shape=(
            shaped((n_ct, 128, 128), BF16),
            shaped((8, SLOTS), I32),
            shaped((8, SLOTS), I32),
        ),
        in_specs=[spec()] * 4,
        out_specs=(hbm, spec(), spec()),
        scratch_shapes=[
            VMEM((4, 128, 128), BF16),
            dma(20),
            dma(20),
            dma(20),
            dma(20),
            pltpu.SemaphoreType.DMA,
        ],
        compiler_params=remote_params(0),
        name="gather_sources",
    )(features, deg_s, rows, cols)

    smem = spec(pltpu.SMEM)
    block = (4, 128, 128)
    return pl.pallas_call(
        functools.partial(main_kernel, (512 * n_row * n_col) ** -0.5, n_row, n_col),
        out_shape=(
            shaped((512, 256), BF16),
            shaped((512, 128), F32),
            shaped((128, 256), F32),
        ),
        in_specs=[smem, smem, spec(), hbm, spec(), spec(), spec(), spec()],
        out_specs=(spec(), spec(), spec()),
        scratch_shapes=[
            VMEM((776, 16, 128), I32),
            VMEM((128, 128), F32),
            VMEM((EMPTY + 8, 128, 128), F32),
            VMEM((n_rt, 128, 128), BF16),
            VMEM(block, BF16),
            VMEM((7,) + block, BF16),
            VMEM((7,) + block, BF16),
            VMEM((8,) + block, BF16),
            VMEM((8,) + block, BF16),
            VMEM((7,) + block, BF16),
            VMEM((7,) + block, BF16),
            VMEM((128, 256), F32),
            VMEM((n_row, 8, 256), F32),
            VMEM((8, 256), F32),
            VMEM((n_col, 8, 256), F32),
            VMEM((128, 256), F32),
            dma(16),
            dma(16),
            dma(20),
            dma(20),
            dma(8),
            dma(8),
            dma(16),
            dma(16),
            dma(n_row),
            dma(n_row),
            dma(n_col),
            dma(n_col),
            dma(n_row),
            dma(n_row),
            pltpu.SemaphoreType.DMA,
            pltpu.SemaphoreType.DMA,
        ],
        compiler_params=remote_params(1),
        name="layer",
    )(fwd_list, bwd_list, gathered, masks, weight, deg_t, deg_s, cotangent)


def solution(mesh):
    in_specs = (
        P(("col", "row"), None),
        P(),
        P(),
        P("row", "col", None),
        P("row", "col", None),
        P("row", "col", None, None, None),
        P(("row", "col"), None),
    )
    out_specs = (P(("row", "col"), None), P(("col", "row"), None), P())
    return jax.shard_map(body, mesh=mesh, in_specs=in_specs, out_specs=out_specs, check_vma=False)
```

time: 121 us -> 102 us (0.84)
  Pallas kernels: 115 us -> 94.5 us
    pallas_call x4 -> x1, Pallas kernels: 95.3 us -> 73 us  [body(): pl.pallas_call(functools.partial(main_kernel, (512 * n_row * n_col) ** (-...]
    pallas_call x1, Pallas kernels: 19.6 us -> 21.5 us  [body(): pl.pallas_call(gather_kernel, out_shape=(shaped((n_ct, 128, 128), BF16),...]
    unnamed x13 -> x3, local copies, waits for them, and re-layouts: 4.35 us -> 4.91 us
where the time goes in v3:
time: 102 us; the launch traced here: 101 us
  Pallas kernels  94.5 us (93%)
  local copies, waits for them, and re-layouts  6.19 us (6%)
    pallas_call x1, Pallas kernels, body(): pl.pallas_call(functools.partial(main_kernel, (512 * n_row * n_col) ** (-...  73 us
    pallas_call x1, Pallas kernels, body(): pl.pallas_call(gather_kernel, out_shape=(shaped((n_ct, 128, 128), BF16),...  21.5 us
    unnamed x3, local copies, waits for them, and re-layouts  4.91 us

profile of v3, /device:TPU:1, one launch (start us, length us, event | category | flops | bytes accessed | tf_op | source)
XLA Modules:
  0.0 101.4 jit_solution(17125169677809364956)
XLA Ops:
  0.6 1.3 %dynamic-slice_bitcast_fusion = (s32[4,128]{1,0:T(4,128)}, s32[4,128]{1,0:T(4,128)}) fusion(s32[128,4,128]{2,1,0:T(4,128)} %bitcast.11, s32[]{:T(128)S(6)} %select_n.8, s32[]{:T(128)S(6)} %select_n.7), kind=kLoop, calls=%fused_computation | loop fusion | bytes 8200 | tf_op jit(solution)/shard_map/jit(dynamic_index_in_dim)/squeeze | solution.py:549
  1.9 21.5 %gather_sources.1 = (bf16[64,128,128]{2,1,0:T(8,128)(2,1)}, s32[8,1024]{1,0:T(8,128)}, s32[8,1024]{1,0:T(8,128)}) custom-call(bf16[512,128]{1,0:T(8,128)(2,1)} %feat.1, s32[4,128]{1,0:T(4,128)} %get-tuple-element.10.deg.deg_s, s32[1,768]{1,0:T(1,128)} %bitcast.9, s32[1,768]{1,0:T(1,128)} %bitcast.10), custom_call_target="tpu_custom_call" | custom-call | tf_op jit(solution)/shard_map/gather_sources/pallas_call | solution.py:556
  23.4 73.0 %layer.1 = (bf16[512,256]{1,0:T(8,128)(2,1)}, f32[512,128]{1,0:T(8,128)}, f32[128,256]{1,0:T(8,128)}) custom-call(s32[8,1024]{1,0:T(8,128)} %get-tuple-element.6.fwd, s32[8,1024]{1,0:T(8,128)} %get-tuple-element.7.bwd, bf16[64,128,128]{2,1,0:T(8,128)(2,1)} %get-tuple-element.8.src, s32[768,16,128]{2,1,0:T(8,128)} %bitcast.8, bf16[128,256]{1,0:T(8,128)(2,1)} %weight.1, ...), custom_call_target="tpu_custom_call" | custom-call | tf_op jit(solution)/shard_map/layer/pallas_call | solution.py:579
  96.5 1.7 %copy.13 = bf16[512,256]{1,0:T(8,128)(2,1)} copy(bf16[512,256]{1,0:T(8,128)(2,1)} %get-tuple-element.14) | data formatting | bytes 524288
  98.1 1.7 %copy.14 = f32[512,128]{1,0:T(8,128)} copy(f32[512,128]{1,0:T(8,128)} %get-tuple-element.15) | data formatting | bytes 524288
  99.8 1.6 %copy.15 = f32[128,256]{1,0:T(8,128)} copy(f32[128,256]{1,0:T(8,128)} %get-tuple-element.16) | data formatting | bytes 262144

commit v4 on v3

--- a/solution.py
+++ b/solution.py
@@ -1,5 +1,4 @@
 import functools
-import itertools
 
 import jax
 import jax.numpy as jnp
@@ -18,9 +17,10 @@
 COL_BITS = 6
 CODE_BITS = ROW_BITS + COL_BITS
 FRESH = 24
-GROUP, UNROLL = 4, 16
-FWD_ROUNDS, BWD_ROUNDS = 14, 15
-EMPTY = BWD_ROUNDS * UNROLL
+GROUP = 4
+FWD_ROUNDS, FWD_UNROLL = 8, 27
+BWD_ROUNDS, BWD_UNROLL = 8, 30
+EMPTY = BWD_ROUNDS * BWD_UNROLL
 BIG = 56 * 1024 * 1024
 
 
@@ -127,124 +127,126 @@
     pltpu.make_async_copy(ref, ref, sem).wait()
 
 
+NAMES = ["x", "om", "op", "o2", "xm", "xp", "x2"]
+
+
+ROUTES = (("x", "op"), ("x", "om"))
+SOURCE = {"x": "o2", "op": "xm", "om": "xp"}
+
+
 def together(*parts):
-    for _ in itertools.zip_longest(*parts):
+    for steps in zip(*parts):
         pass
 
 
-PIECES = [
-    ("x", 0, 2), ("om", 0, 2), ("op", 0, 2), ("o2", 0, 1), ("o2", 1, 1),
-    ("xm", 0, 2), ("xp", 0, 2), ("x2", 0, 1), ("x2", 1, 1), ("o", 0, 2),
-]
-
-
-def spread(place, mine, out, sems, twin_sems, chunk, sent):
-    low = 10 * chunk
-
-    def part(index, first, tiles):
+def spread_start(place, mine, out, sems, twin_sems, chunk, sent):
+    own = mine.at[pl.ds(2 * chunk, 2)]
+    here = out.at[pl.ds(place.index("o") * 4 + 2 * chunk, 2)]
+    for i, to in enumerate(("x", "op", "om")):
+        sent.append(send(own, here, sems, 8 * chunk + i, place.device(to)))
+    if place.core is not None:
+        sent.append(send(own, here, twin_sems, 8 * chunk + 7, place.device("twin")))
+
+
+def spread(place, out, sems, twin_sems, chunk, sent):
+    low = 8 * chunk
+
+    def part(index, first=0, tiles=2):
         return out.at[pl.ds(index * 4 + 2 * chunk + first, tiles)]
 
-    def region(i):
-        name, first, tiles = PIECES[i]
-        return part(place.index(name), first, tiles)
-
-    def pass_on(i, to, dst, src):
-        sent.append(send(src, dst, sems, low + i, place.device(to)))
-
-    def twin(i, src):
+    def wait(i, name, first=0, tiles=2):
+        landed(part(place.index(name), first, tiles), sems[1].at[low + i])
+
+    def pass_on(i, to, name, first=0, tiles=2):
+        ref = part(place.index(name), first, tiles)
+        sent.append(send(ref, ref, sems, low + i, place.device(to)))
+
+    def twin(*names):
         if place.core is not None:
-            sent.append(send(src, region(i), twin_sems, low + i, place.device("twin")))
-
-    own = mine.at[pl.ds(2 * chunk, 2)]
-    for i, to in ((0, "x"), (1, "op"), (2, "om")):
-        pass_on(i, to, region(9), own)
-    twin(9, own)
-    yield
-
-    def forward(i, targets):
-        ref = region(i)
-        landed(ref, sems[1].at[low + i])
-        for j, to in targets:
-            pass_on(j, to, ref, ref)
-        twin(i, ref)
-
-    def forward_half(i, j, to):
-        landed(region(i), sems[1].at[low + i])
-        half = part(place.index(PIECES[i][0]), PIECES[j][1], 1)
-        pass_on(j, to, half, half)
-        twin(i, region(i))
-
-    forward(0, ((5, "op"), (6, "om")))
-    yield
-    forward_half(1, 3, "op")
-    yield
-    forward_half(2, 4, "om")
-    yield
-    forward(3, ((7, "x"),))
-    yield
-    forward(4, ((8, "x"),))
-    yield
-    for i in (5, 6, 7, 8):
-        forward(i, ())
-        yield
+            for name in names:
+                ref = part(place.index(name))
+                i = low + NAMES.index(name)
+                sent.append(send(ref, ref, twin_sems, i, place.device("twin")))
+
+    wait(0, "x")
+    pass_on(3, "op", "x")
+    wait(2, "op")
+    pass_on(4, "x", "op")
+    pass_on(5, "om", "op")
+    wait(1, "om")
+    twin("x", "op", "om")
+    yield
+    wait(3, "xm")
+    wait(4, "xp")
+    wait(5, "o2")
+    for t, to in enumerate(ROUTES[chunk]):
+        pass_on(6 + t, to, SOURCE[to], t, 1)
+    twin("xm", "xp", "o2")
+    yield
+    for t in range(2):
+        wait(6 + t, "x2", t, 1)
+    twin("x2")
+    yield
     if place.core is not None:
-        for i in range(10):
-            name, first, tiles = PIECES[i]
-            ref = part(place.chip(name) * 2 + 1 - place.core, first, tiles)
-            landed(ref, twin_sems[1].at[low + i])
+        for i, name in enumerate(NAMES + ["o"]):
+            index = place.chip(name) * 2 + 1 - place.core
+            landed(part(index), twin_sems[1].at[low + i])
+    yield
 
 
 def gather_up(place, ready, value, staged, got, sems, chunk, sent):
     low = 8 * chunk
-    t0, t1 = 2 * chunk, 2 * chunk + 1
-    both = pl.ds(t0, 2)
-
-    def go(i, slot, into, at, to):
-        src, dst = staged.at[slot, at], got.at[into, at]
-        sent.append(send(src, dst, sems, low + i, place.device(to)))
-
-    def wait(i, into, at=both):
-        landed(got.at[into, at], sems[1].at[low + i])
-
-    def stage(name, slot, tiles, *slots):
-        for t in tiles:
+    both = (2 * chunk, 2 * chunk + 1)
+
+    def go(i, slot, into, to, tiles=both):
+        at = pl.ds(tiles[0], len(tiles))
+        sent.append(send(staged.at[slot, at], got.at[into, at], sems, low + i, place.device(to)))
+
+    def wait(i, into, tiles=both):
+        landed(got.at[into, pl.ds(tiles[0], len(tiles))], sems[1].at[low + i])
+
+    def stage(name, slot, *added):
+        ready(name)
+        for t in both:
             total = value(name, t)
-            for k in slots:
-                total = total + got[k, t].astype(F32)
+            for into, tiles in added:
+                if t in tiles:
+                    total = total + got[into, t].astype(F32)
             staged[slot, t] = total.astype(BF16)
 
-    for i, name, to in ((0, "x2", "x"), (1, "xm", "om"), (2, "xp", "op")):
-        ready(name)
-        stage(name, i, (t0, t1))
-        go(i, i, i, both, to)
-    yield
-    wait(0, 0)
-    ready("o2")
-    stage("o2", 3, (t0, t1), 0)
-    go(3, 3, 3, pl.ds(t0, 1), "om")
-    go(4, 3, 3, pl.ds(t1, 1), "op")
-    yield
-    wait(1, 1)
-    wait(2, 2)
-    ready("x")
-    stage("x", 4, (t0, t1), 1, 2)
-    go(5, 4, 4, both, "x")
-    yield
-    ready("om")
-    wait(3, 3, pl.ds(t0, 1))
-    stage("om", 5, (t0,), 3)
-    stage("om", 5, (t1,))
-    go(6, 5, 5, both, "om")
-    yield
-    ready("op")
-    wait(4, 3, pl.ds(t1, 1))
-    stage("op", 6, (t1,), 3)
-    stage("op", 6, (t0,))
-    go(7, 6, 6, both, "op")
+    stage("x2", 0)
+    go(0, 0, 0, "x", both[:1])
+    go(1, 0, 0, ("om", "op")[chunk], both[1:])
+    stage("om", 6)
+    go(2, 6, 5, "om")
+    yield
+    if chunk == 0:
+        stage("xp", 1)
+        go(3, 1, 1, "x")
+        wait(1, 0, both[1:])
+        stage("xm", 2, (0, both[1:]))
+        go(4, 2, 2, "om")
+    else:
+        stage("xm", 2)
+        go(4, 2, 2, "om")
+        wait(1, 0, both[1:])
+        stage("xp", 1, (0, both[1:]))
+        go(3, 1, 1, "x")
+    wait(0, 0, both[:1])
+    stage("o2", 3, (0, both[:1]))
+    go(5, 3, 3, "op")
+    yield
+    wait(4, 2)
+    stage("x", 4, (2, both))
+    go(6, 4, 4, "x")
+    wait(3, 1)
+    wait(5, 3)
+    stage("op", 5, (1, both), (3, both))
+    go(7, 5, 6, "op")
     yield
     ready("o")
-    for i in (4, 5, 6):
-        wait(i + 1, i)
+    for i, into in ((2, 5), (6, 4), (7, 6)):
+        wait(i, into)
     yield
 
 
@@ -293,11 +295,19 @@
 
 
 def gather_kernel(
-    feat, deg, rows, cols, out, fwd_list, bwd_list, mine, s1, r1, s2, r2, own_sem
+    feat, degrees_all, rows, cols, out, fwd_list, bwd_list, mine, deg, s1, r1, s2, r2, own_sem, deg_sem
 ):
     place = Place("row")
+    chip_block = lax.axis_index("col") * lax.axis_size("row") + lax.axis_index("row")
+    load = pltpu.make_async_copy(degrees_all.at[chip_block], deg, deg_sem)
+    load.start()
+    barrier = pltpu.get_barrier_semaphore()
+    partners = ["x", "om", "op", "twin"]
+    for name in partners:
+        pl.semaphore_signal(barrier, inc=1, device_id=place.device(name), device_id_type=MESH)
     lane = iota((128, 128), 1)
     perm = (iota((128, 128), 0) == ((lane & 15) * 8 + (lane >> 4))).astype(F32).astype(BF16)
+    load.wait()
     degrees = mm(deg[...].astype(F32).astype(BF16), perm)
     bucket = iota((1, 128), 1) >> 4
     shrink = jnp.zeros((1, 128), F32)
@@ -309,22 +319,17 @@
             feat[t * 128 : (t + 1) * 128, :], perm, (((0,), (0,)), ((), ())), preferred_element_type=F32
         )
         mine[t] = (turned * inverse[t : t + 1, :] * shrink).astype(BF16)
-    barrier = pltpu.get_barrier_semaphore()
-    partners = ["x", "om", "op", "twin"]
-    for name in partners:
-        pl.semaphore_signal(barrier, inc=1, device_id=place.device(name), device_id_type=MESH)
     pl.semaphore_wait(barrier, len(partners))
     sent = []
-    chunks = [spread(place, mine, out, (s1, r1), (s2, r2), c, sent) for c in range(2)]
-    for chunk in chunks:
-        next(chunk)
+    for c in range(2):
+        spread_start(place, mine, out, (s1, r1), (s2, r2), c, sent)
     own = pltpu.make_async_copy(mine, out.at[pl.ds(place.index("o") * 4, 4)], own_sem)
     own.start()
     r, c = rows[...], cols[...]
     fwd_list[...] = order_list(r, r, c, 1 << ROW_BITS, GROUP)
     bwd_list[...] = order_list(c, r, c, 1 << COL_BITS, GROUP)
     own.wait()
-    together(*chunks)
+    together(*[spread(place, out, (s1, r1), (s2, r2), c, sent) for c in range(2)])
     for copy in sent:
         copy.wait_send()
 
@@ -335,34 +340,38 @@
     return jnp.concatenate(parts, axis=1)
 
 
-def run_tiles(rounds, codes, product, acc, run):
-    acc[...] = jnp.zeros_like(acc)
-
+def run_tiles(start, stop, unroll, codes, product, acc, run):
     def body(i, carry):
         total = acc[...]
-        for u in range(UNROLL):
-            at = (i * UNROLL + u) * GROUP
+        for u in range(unroll):
+            at = (i * unroll + u) * GROUP
             code = [codes[0, at + g] for g in range(GROUP)]
             keep = (1 - ((code[0] >> FRESH) & 1)).astype(F32)
             total = total * keep + product(code)
-            run[i * UNROLL + u] = total
+            run[i * unroll + u] = total
         acc[...] = total
         return carry
 
-    lax.fori_loop(0, rounds, body, 0)
+    lax.fori_loop(start, stop, body, 0)
 
 
 def main_kernel(
-    scale, n_row, n_col, fwd, bwd, src, masks, weight, deg_t, deg_s, cot, act, out, gw_out,
-    held, acc, run, targets, mine, staged_c, got_c, twin_out, from_twin, staged_r, got_r,
+    scale, n_row, n_col, fwd, bwd, src, masks, weight, degrees_all, cot, act, out, gw_out,
+    deg_t, deg_s, held, acc, run, targets, mine, staged_c, got_c, twin_out, from_twin, staged_r, got_r,
     gw, gw_got, gw_row, gw_col, gw_all,
-    sc, rc, sg, rg, s0, r0, sr, rr, s2, r2, s3, r3, s4, r4, mask_sem, own_sem,
+    sc, rc, sg, rg, s0, r0, sr, rr, s2, r2, s3, r3, s4, r4, mask_sem, own_sem, deg_sem,
 ):
     row = lax.axis_index("row")
     col = lax.axis_index("col")
     rows_place, cols_place = Place("row"), Place("col")
     load = pltpu.make_async_copy(masks, held.at[pl.ds(0, 768)], mask_sem)
     load.start()
+    loads = [
+        pltpu.make_async_copy(degrees_all.at[row * n_col + col], deg_t, deg_sem.at[0]),
+        pltpu.make_async_copy(degrees_all.at[col * n_row + row], deg_s, deg_sem.at[1]),
+    ]
+    for copy in loads:
+        copy.start()
     barrier = pltpu.get_barrier_semaphore()
 
     def row_peer(step):
@@ -378,6 +387,8 @@
     held[768] = jnp.zeros((16, 128), I32)
     run[EMPTY] = jnp.zeros((128, 128), F32)
     load.wait()
+    for copy in loads:
+        copy.wait()
 
     def forward(code):
         lhs = jnp.concatenate(
@@ -385,7 +396,8 @@
         )
         return mm(lhs, unpack(held, code).reshape(GROUP * 128, 128))
 
-    run_tiles(FWD_ROUNDS, fwd, forward, acc, run)
+    acc[...] = jnp.zeros_like(acc)
+    run_tiles(0, FWD_ROUNDS, FWD_UNROLL, fwd, forward, acc, run)
     pl.semaphore_wait(barrier, n_row + n_col - 2)
     sent = []
 
@@ -396,13 +408,12 @@
         gather_up(cols_place, lambda name: None, forward_sum, staged_c, got_c, (sc, rc), c, sent)
         for c in range(2)
     ]
-    for _ in range(5):
+    for _ in range(3):
         for up in ups:
             next(up)
     w = weight[...]
     inverse = lax.rsqrt(deg_t[...].astype(F32))
     total = jnp.zeros((128, 256), F32)
-    downs = []
     for c in range(2):
         next(ups[c])
         for t in (2 * c, 2 * c + 1):
@@ -424,12 +435,12 @@
             mine[t] = lax.dot_general(
                 scaled, w, (((1,), (1,)), ((), ())), preferred_element_type=F32
             ).astype(BF16)
-        down = spread(cols_place, mine, targets, (sg, rg), None, c, sent)
-        next(down)
-        downs.append(down)
+        spread_start(cols_place, mine, targets, (sg, rg), None, c, sent)
     own = pltpu.make_async_copy(mine, targets.at[pl.ds(col * 4, 4)], own_sem)
     own.start()
     gw[...] = total * scale
+    own.wait()
+    together(*[spread(cols_place, targets, (sg, rg), None, c, sent) for c in range(2)])
     weights = [
         send(
             gw.at[pl.ds(lax.rem(row + step, n_row) * 8, 8)],
@@ -440,24 +451,14 @@
         )
         for step in range(1, n_row)
     ]
-    own.wait()
-    together(*downs)
 
     def backward(code):
         rhs = jnp.concatenate([targets[k & ((1 << ROW_BITS) - 1)] for k in code], axis=0)
         tiles = unpack(held, code)
         return mm(jnp.concatenate([tiles[g] for g in range(GROUP)], axis=1), rhs)
 
-    run_tiles(BWD_ROUNDS, bwd, backward, acc, run)
-
-    order = ["x2", "xm", "xp", "o2", "x", "om", "op", "o"]
-    for k, name in enumerate(order):
-        index = rows_place.chip(name) * 2 + 1 - rows_place.core
-        for t in range(4):
-            twin_out[k, t] = run[bwd[1, index * 4 + t]].astype(BF16)
-        sent.append(
-            send(twin_out.at[k], from_twin.at[k], (s0, r0), k, rows_place.device("twin"))
-        )
+    acc[...] = jnp.zeros_like(acc)
+    run_tiles(0, BWD_ROUNDS // 2, BWD_UNROLL, bwd, backward, acc, run)
     for copy in weights:
         copy.wait()
     summed = gw[pl.ds(row * 8, 8), :]
@@ -467,7 +468,16 @@
     gw_col[pl.ds(col, 1)] = summed[None]
     for step in range(1, n_col):
         sent.append(send(gw_row, gw_col.at[col], (s3, r3), step, col_peer(step)))
-
+    run_tiles(BWD_ROUNDS // 2, BWD_ROUNDS, BWD_UNROLL, bwd, backward, acc, run)
+
+    order = ["x2", "om", "xp", "xm", "o2", "x", "op", "o"]
+    for k, name in enumerate(order):
+        index = rows_place.chip(name) * 2 + 1 - rows_place.core
+        for t in range(4):
+            twin_out[k, t] = run[bwd[1, index * 4 + t]].astype(BF16)
+        sent.append(
+            send(twin_out.at[k], from_twin.at[k], (s0, r0), k, rows_place.device("twin"))
+        )
     arrived = set()
 
     def ready(name):
@@ -484,9 +494,8 @@
         gather_up(rows_place, ready, backward_sum, staged_r, got_r, (sr, rr), c, sent)
         for c in range(2)
     ]
-    for _ in range(4):
-        for up in ups:
-            next(up)
+    for up in ups:
+        next(up)
     for step in range(1, n_col):
         landed(gw_col.at[lax.rem(col + n_col - step, n_col)], r3.at[step])
     summed = gw_col[0]
@@ -496,21 +505,22 @@
     gw_all[pl.ds(row * 8, 8), :] = summed
     weights = [send(gw_mine, gw_mine, (s4, r4), step, row_peer(step)) for step in range(1, n_row)]
     inverse = lax.rsqrt(deg_s[...].astype(F32))
-    for up in ups:
-        next(up)
+    for _ in range(2):
+        for up in ups:
+            next(up)
     bucket = iota((128, 128), 0) >> 4
     grow = jnp.zeros((128, 128), F32)
     for b in range(8):
         grow = jnp.where(bucket == b, 2.0**-b, grow)
-    for c in range(2):
-        next(ups[c])
-        for t in (2 * c, 2 * c + 1):
-            factor = jnp.broadcast_to(inverse[t : t + 1, :], (128, 128)).T
-            summed = gathered_tile(backward_sum, got_r, t) * grow
-            for b in range(8):
-                out[pl.ds(t * 128 + b, 16, stride=8), :] = summed[b * 16 : (b + 1) * 16, :]
-            rows = pl.ds(t * 128, 128)
-            out[rows, :] = out[rows, :] * factor
+    for t in range(4):
+        if t % 2 == 0:
+            next(ups[t // 2])
+        factor = jnp.broadcast_to(inverse[t : t + 1, :], (128, 128)).T
+        summed = gathered_tile(backward_sum, got_r, t) * grow
+        for b in range(8):
+            out[pl.ds(t * 128 + b, 16, stride=8), :] = summed[b * 16 : (b + 1) * 16, :]
+        rows = pl.ds(t * 128, 128)
+        out[rows, :] = out[rows, :] * factor
     for copy in sent:
         copy.wait_send()
     for copy in weights:
@@ -521,6 +531,12 @@
     gw_out[...] = gw_all[...]
 
 
+def hand_on_kernel(a, b, c, a_out, b_out, c_out):
+    a_out[...] = a[...]
+    b_out[...] = b[...]
+    c_out[...] = c[...]
+
+
 def spec(space=VMEM):
     return pl.BlockSpec(memory_space=space)
 
@@ -540,13 +556,9 @@
 
 
 def body(features, weight, degrees, tile_rows, tile_cols, tile_masks, cotangent):
-    row = lax.axis_index("row")
-    col = lax.axis_index("col")
     n_row = lax.axis_size("row")
     n_col = lax.axis_size("col")
     deg = degrees.reshape(n_row * n_col, 4, 128)
-    deg_s = lax.dynamic_index_in_dim(deg, col * n_row + row, 0, False)
-    deg_t = lax.dynamic_index_in_dim(deg, row * n_col + col, 0, False)
     rows = tile_rows.reshape(1, -1)
     cols = tile_cols.reshape(1, -1)
     masks = tile_masks.reshape(-1, 16, 128)
@@ -560,32 +572,37 @@
             shaped((8, SLOTS), I32),
             shaped((8, SLOTS), I32),
         ),
-        in_specs=[spec()] * 4,
+        in_specs=[spec(), hbm, spec(), spec()],
         out_specs=(hbm, spec(), spec()),
         scratch_shapes=[
             VMEM((4, 128, 128), BF16),
-            dma(20),
-            dma(20),
-            dma(20),
-            dma(20),
+            VMEM((4, 128), I32),
+            dma(16),
+            dma(16),
+            dma(16),
+            dma(16),
+            pltpu.SemaphoreType.DMA,
             pltpu.SemaphoreType.DMA,
         ],
         compiler_params=remote_params(0),
         name="gather_sources",
-    )(features, deg_s, rows, cols)
+    )(features, deg, rows, cols)
 
     smem = spec(pltpu.SMEM)
+    outs = (
+        shaped((512, 256), BF16),
+        shaped((512, 128), F32),
+        shaped((128, 256), F32),
+    )
     block = (4, 128, 128)
-    return pl.pallas_call(
+    results = pl.pallas_call(
         functools.partial(main_kernel, (512 * n_row * n_col) ** -0.5, n_row, n_col),
-        out_shape=(
-            shaped((512, 256), BF16),
-            shaped((512, 128), F32),
-            shaped((128, 256), F32),
-        ),
-        in_specs=[smem, smem, spec(), hbm, spec(), spec(), spec(), spec()],
+        out_shape=outs,
+        in_specs=[smem, smem, spec(), hbm, spec(), hbm, spec()],
         out_specs=(spec(), spec(), spec()),
         scratch_shapes=[
+            VMEM((4, 128), I32),
+            VMEM((4, 128), I32),
             VMEM((776, 16, 128), I32),
             VMEM((128, 128), F32),
             VMEM((EMPTY + 8, 128, 128), F32),
@@ -604,8 +621,8 @@
             VMEM((128, 256), F32),
             dma(16),
             dma(16),
-            dma(20),
-            dma(20),
+            dma(16),
+            dma(16),
             dma(8),
             dma(8),
             dma(16),
@@ -618,10 +635,18 @@
             dma(n_row),
             pltpu.SemaphoreType.DMA,
             pltpu.SemaphoreType.DMA,
+            dma(2),
         ],
         compiler_params=remote_params(1),
         name="layer",
-    )(fwd_list, bwd_list, gathered, masks, weight, deg_t, deg_s, cotangent)
+    )(fwd_list, bwd_list, gathered, masks, weight, deg, cotangent)
+    return pl.pallas_call(
+        hand_on_kernel,
+        out_shape=outs,
+        in_specs=[spec()] * 3,
+        out_specs=(spec(), spec(), spec()),
+        name="results",
+    )(*results)
 
 
 def solution(mesh):

time: 102 us -> 93.4 us (0.916)
  local copies, waits for them, and re-layouts: 6.19 us -> 0 us
  Pallas kernels: 94.5 us -> 92.6 us
    unnamed x3 -> x0, local copies, waits for them, and re-layouts: 4.91 us -> none
    pallas_call x1, Pallas kernels: 73 us -> 70.5 us  [body(): pl.pallas_call(functools.partial(main_kernel, (512 * n_row * n_col) ** (-...]
    pallas_call x0 -> x1, Pallas kernels: none -> 1.91 us  [body(): pl.pallas_call(hand_on_kernel, out_shape=outs, in_specs=[spec()] * 3, out...]
    pallas_call x1, Pallas kernels: 21.5 us -> 20.2 us  [body(): pl.pallas_call(gather_kernel, out_shape=(shaped((n_ct, 128, 128), BF16),...]
    squeeze x1 -> x0, local copies, waits for them, and re-layouts: 1.29 us -> none  [body(): deg_t = lax.dynamic_index_in_dim(deg, row * n_col + col, 0, False)]
where the time goes in v4:
time: 93.4 us; the launch traced here: 93.2 us
  Pallas kernels  92.6 us (99%)
    pallas_call x1, Pallas kernels, body(): pl.pallas_call(functools.partial(main_kernel, (512 * n_row * n_col) ** (-...  70.5 us
    pallas_call x1, Pallas kernels, body(): pl.pallas_call(gather_kernel, out_shape=(shaped((n_ct, 128, 128), BF16),...  20.2 us
    pallas_call x1, Pallas kernels, body(): pl.pallas_call(hand_on_kernel, out_shape=outs, in_specs=[spec()] * 3, out...  1.91 us

profile of v4, /device:TPU:1, one launch (start us, length us, event | category | flops | bytes accessed | tf_op | source)
XLA Modules:
  0.0 93.2 jit_solution(9372734524029762793)
XLA Ops:
  0.6 20.2 %gather_sources.1 = (bf16[64,128,128]{2,1,0:T(8,128)(2,1)}, s32[8,1024]{1,0:T(8,128)}, s32[8,1024]{1,0:T(8,128)}) custom-call(bf16[512,128]{1,0:T(8,128)(2,1)} %feat.1, s32[128,4,128]{2,1,0:T(4,128)} %bitcast.5, s32[1,768]{1,0:T(1,128)} %bitcast.7, s32[1,768]{1,0:T(1,128)} %bitcast.8), custom_call_target="tpu_custom_call" | custom-call | tf_op jit(solution)/shard_map/gather_sources/pallas_call | solution.py:568
  20.8 70.5 %layer.1 = (bf16[512,256]{1,0:T(8,128)(2,1)}, f32[512,128]{1,0:T(8,128)}, f32[128,256]{1,0:T(8,128)}) custom-call(s32[8,1024]{1,0:T(8,128)} %get-tuple-element.9.fwd, s32[8,1024]{1,0:T(8,128)} %get-tuple-element.10.bwd, bf16[64,128,128]{2,1,0:T(8,128)(2,1)} %get-tuple-element.11.src, s32[768,16,128]{2,1,0:T(8,128)} %bitcast.4, bf16[128,256]{1,0:T(8,128)(2,1)} %weight.1, ...), custom_call_target="tpu_custom_call" | custom-call | tf_op jit(solution)/shard_map/layer/pallas_call | solution.py:598
  91.3 1.9 %results.1 = (bf16[512,256]{1,0:T(8,128)(2,1)}, f32[512,128]{1,0:T(8,128)}, f32[128,256]{1,0:T(8,128)}) custom-call(bf16[512,256]{1,0:T(8,128)(2,1)} %get-tuple-element.12.a, f32[512,128]{1,0:T(8,128)} %get-tuple-element.13.b, f32[128,256]{1,0:T(8,128)} %get-tuple-element.14.c), custom_call_target="tpu_custom_call" | custom-call | tf_op jit(solution)/shard_map/results/pallas_call | solution.py:643

commit v5 on v4

--- a/solution.py
+++ b/solution.py
@@ -294,20 +294,9 @@
     return jnp.where(iota((8, SLOTS), 0) == 0, code, last.astype(I32))
 
 
-def gather_kernel(
-    feat, degrees_all, rows, cols, out, fwd_list, bwd_list, mine, deg, s1, r1, s2, r2, own_sem, deg_sem
-):
-    place = Place("row")
-    chip_block = lax.axis_index("col") * lax.axis_size("row") + lax.axis_index("row")
-    load = pltpu.make_async_copy(degrees_all.at[chip_block], deg, deg_sem)
-    load.start()
-    barrier = pltpu.get_barrier_semaphore()
-    partners = ["x", "om", "op", "twin"]
-    for name in partners:
-        pl.semaphore_signal(barrier, inc=1, device_id=place.device(name), device_id_type=MESH)
+def scale_sources(feat, deg, mine):
     lane = iota((128, 128), 1)
     perm = (iota((128, 128), 0) == ((lane & 15) * 8 + (lane >> 4))).astype(F32).astype(BF16)
-    load.wait()
     degrees = mm(deg[...].astype(F32).astype(BF16), perm)
     bucket = iota((1, 128), 1) >> 4
     shrink = jnp.zeros((1, 128), F32)
@@ -318,26 +307,19 @@
         turned = lax.dot_general(
             feat[t * 128 : (t + 1) * 128, :], perm, (((0,), (0,)), ((), ())), preferred_element_type=F32
         )
-        mine[t] = (turned * inverse[t : t + 1, :] * shrink).astype(BF16)
-    pl.semaphore_wait(barrier, len(partners))
-    sent = []
-    for c in range(2):
-        spread_start(place, mine, out, (s1, r1), (s2, r2), c, sent)
-    own = pltpu.make_async_copy(mine, out.at[pl.ds(place.index("o") * 4, 4)], own_sem)
-    own.start()
-    r, c = rows[...], cols[...]
-    fwd_list[...] = order_list(r, r, c, 1 << ROW_BITS, GROUP)
-    bwd_list[...] = order_list(c, r, c, 1 << COL_BITS, GROUP)
-    own.wait()
-    together(*[spread(place, out, (s1, r1), (s2, r2), c, sent) for c in range(2)])
-    for copy in sent:
-        copy.wait_send()
+        factor = inverse[t : t + 1, :] * shrink
+        mine[t] = (turned * factor).astype(BF16)
+    return [inverse[t : t + 1, :] * shrink for t in range(4)]
 
 
 def unpack(held, codes):
-    words = jnp.concatenate([held[pl.ds((k >> CODE_BITS) & 1023, 1)] for k in codes], axis=0)
+    words = jnp.concatenate([held[pl.ds(jnp.minimum((k >> CODE_BITS) & 1023, 768), 1)] for k in codes], axis=0)
     parts = [(words & (1 << b)).astype(F32).astype(BF16) for b in range(8)]
     return jnp.concatenate(parts, axis=1)
+
+
+def entry(codes, key):
+    return jnp.clip(codes[1, key], 0, EMPTY)
 
 
 def run_tiles(start, stop, unroll, codes, product, acc, run):
@@ -356,10 +338,10 @@
 
 
 def main_kernel(
-    scale, n_row, n_col, fwd, bwd, src, masks, weight, degrees_all, cot, act, out, gw_out,
-    deg_t, deg_s, held, acc, run, targets, mine, staged_c, got_c, twin_out, from_twin, staged_r, got_r,
-    gw, gw_got, gw_row, gw_col, gw_all,
-    sc, rc, sg, rg, s0, r0, sr, rr, s2, r2, s3, r3, s4, r4, mask_sem, own_sem, deg_sem,
+    scale, n_row, n_col, rows, cols, feat, masks, weight, degrees_all, cot, act, out, gw_out,
+    fwd, bwd, fwd_list, bwd_list, out_factor, back_factor, deg_t, deg_s, src, source, held, acc, run, targets, mine, staged_c, got_c, twin_out, from_twin, staged_r, got_r,
+    agg_hold, grad_hold, gw, gw_got, gw_row, gw_col, gw_all,
+    sa, ra, st, rt, sc, rc, sg, rg, s0, r0, sr, rr, s2, r2, s3, r3, s4, r4, mask_sem, own_sem, deg_sem, list_sem,
 ):
     row = lax.axis_index("row")
     col = lax.axis_index("col")
@@ -386,8 +368,32 @@
         pl.semaphore_signal(barrier, inc=1, device_id=col_peer(step), device_id_type=MESH)
     held[768] = jnp.zeros((16, 128), I32)
     run[EMPTY] = jnp.zeros((128, 128), F32)
+    for copy in loads:
+        copy.wait()
+    back_factors = scale_sources(feat, deg_s, source)
+    own = pltpu.make_async_copy(source, src.at[pl.ds(rows_place.index("o") * 4, 4)], own_sem)
+    own.start()
+    pl.semaphore_wait(barrier, n_row + n_col - 2)
+    sent = []
+    for c in range(2):
+        spread_start(rows_place, source, src, (sa, ra), (st, rt), c, sent)
+    r, c = rows[...], cols[...]
+    fwd_list[...] = order_list(r, r, c, 1 << ROW_BITS, GROUP)
+    bwd_list[...] = order_list(c, r, c, 1 << COL_BITS, GROUP)
+    lists = [
+        pltpu.make_async_copy(fwd_list, fwd, list_sem.at[0]),
+        pltpu.make_async_copy(bwd_list, bwd, list_sem.at[1]),
+    ]
+    for copy in lists:
+        copy.start()
+    inverse = lax.rsqrt(deg_t[...].astype(F32))
+    for t in range(4):
+        back_factor[t] = jnp.broadcast_to(back_factors[t], (128, 128)).T
+        out_factor[t] = jnp.broadcast_to(inverse[t : t + 1, :], (128, 128)).T
+    own.wait()
+    together(*[spread(rows_place, src, (sa, ra), (st, rt), c, sent) for c in range(2)])
     load.wait()
-    for copy in loads:
+    for copy in lists:
         copy.wait()
 
     def forward(code):
@@ -398,11 +404,9 @@
 
     acc[...] = jnp.zeros_like(acc)
     run_tiles(0, FWD_ROUNDS, FWD_UNROLL, fwd, forward, acc, run)
-    pl.semaphore_wait(barrier, n_row + n_col - 2)
-    sent = []
 
     def forward_sum(name, t):
-        return run[fwd[1, cols_place.index(name) * 4 + t]]
+        return run[entry(fwd, cols_place.index(name) * 4 + t)]
 
     ups = [
         gather_up(cols_place, lambda name: None, forward_sum, staged_c, got_c, (sc, rc), c, sent)
@@ -412,25 +416,21 @@
         for up in ups:
             next(up)
     w = weight[...]
-    inverse = lax.rsqrt(deg_t[...].astype(F32))
-    total = jnp.zeros((128, 256), F32)
     for c in range(2):
         next(ups[c])
         for t in (2 * c, 2 * c + 1):
             summed = gathered_tile(forward_sum, got_c, t)
-            factor = jnp.broadcast_to(inverse[t : t + 1, :], (128, 128))
-            agg_t = summed * factor
-            factor = factor.T
+            agg_t = summed * inverse[t : t + 1, :]
+            factor = out_factor[t]
             factor = jnp.concatenate([factor, factor], axis=1)
-            t_hi, t_lo = split(agg_t)
             hi, lo = split(agg_t.T)
             pre = mm(hi, w) + mm(lo, w)
             slope = jnp.where(pre > 0, 1.0, jnp.exp(jnp.minimum(pre, 0.0)))
-            rows = pl.ds(t * 128, 128)
-            act[rows, :] = jnp.where(pre > 0, pre, slope - 1.0).astype(BF16)
-            grad = cot[rows, :].astype(F32) * slope
-            g_hi, g_lo = split(grad)
-            total = total + (mm(t_hi, g_hi) + (mm(t_lo, g_hi) + mm(t_hi, g_lo)))
+            here = pl.ds(t * 128, 128)
+            act[here, :] = jnp.where(pre > 0, pre, slope - 1.0).astype(BF16)
+            grad = cot[here, :].astype(F32) * slope
+            agg_hold[t] = agg_t
+            grad_hold[t] = grad
             scaled = (grad * factor).astype(BF16)
             mine[t] = lax.dot_general(
                 scaled, w, (((1,), (1,)), ((), ())), preferred_element_type=F32
@@ -438,6 +438,11 @@
         spread_start(cols_place, mine, targets, (sg, rg), None, c, sent)
     own = pltpu.make_async_copy(mine, targets.at[pl.ds(col * 4, 4)], own_sem)
     own.start()
+    total = jnp.zeros((128, 256), F32)
+    for t in range(4):
+        t_hi, t_lo = split(agg_hold[t])
+        g_hi, g_lo = split(grad_hold[t])
+        total = total + (mm(t_hi, g_hi) + (mm(t_lo, g_hi) + mm(t_hi, g_lo)))
     gw[...] = total * scale
     own.wait()
     together(*[spread(cols_place, targets, (sg, rg), None, c, sent) for c in range(2)])
@@ -474,7 +479,7 @@
     for k, name in enumerate(order):
         index = rows_place.chip(name) * 2 + 1 - rows_place.core
         for t in range(4):
-            twin_out[k, t] = run[bwd[1, index * 4 + t]].astype(BF16)
+            twin_out[k, t] = run[entry(bwd, index * 4 + t)].astype(BF16)
         sent.append(
             send(twin_out.at[k], from_twin.at[k], (s0, r0), k, rows_place.device("twin"))
         )
@@ -487,7 +492,7 @@
             arrived.add(name)
 
     def backward_sum(name, t):
-        mine_sum = run[bwd[1, rows_place.index(name) * 4 + t]]
+        mine_sum = run[entry(bwd, rows_place.index(name) * 4 + t)]
         return mine_sum + from_twin[order.index(name), t].astype(F32)
 
     ups = [
@@ -504,23 +509,15 @@
     gw_mine = gw_all.at[pl.ds(row * 8, 8)]
     gw_all[pl.ds(row * 8, 8), :] = summed
     weights = [send(gw_mine, gw_mine, (s4, r4), step, row_peer(step)) for step in range(1, n_row)]
-    inverse = lax.rsqrt(deg_s[...].astype(F32))
     for _ in range(2):
         for up in ups:
             next(up)
-    bucket = iota((128, 128), 0) >> 4
-    grow = jnp.zeros((128, 128), F32)
-    for b in range(8):
-        grow = jnp.where(bucket == b, 2.0**-b, grow)
     for t in range(4):
         if t % 2 == 0:
             next(ups[t // 2])
-        factor = jnp.broadcast_to(inverse[t : t + 1, :], (128, 128)).T
-        summed = gathered_tile(backward_sum, got_r, t) * grow
+        summed = gathered_tile(backward_sum, got_r, t) * back_factor[t]
         for b in range(8):
             out[pl.ds(t * 128 + b, 16, stride=8), :] = summed[b * 16 : (b + 1) * 16, :]
-        rows = pl.ds(t * 128, 128)
-        out[rows, :] = out[rows, :] * factor
     for copy in sent:
         copy.wait_send()
     for copy in weights:
@@ -565,30 +562,6 @@
     hbm = spec(pl.ANY)
     n_rt, n_ct = 4 * n_col, 4 * n_row
 
-    gathered, fwd_list, bwd_list = pl.pallas_call(
-        gather_kernel,
-        out_shape=(
-            shaped((n_ct, 128, 128), BF16),
-            shaped((8, SLOTS), I32),
-            shaped((8, SLOTS), I32),
-        ),
-        in_specs=[spec(), hbm, spec(), spec()],
-        out_specs=(hbm, spec(), spec()),
-        scratch_shapes=[
-            VMEM((4, 128, 128), BF16),
-            VMEM((4, 128), I32),
-            dma(16),
-            dma(16),
-            dma(16),
-            dma(16),
-            pltpu.SemaphoreType.DMA,
-            pltpu.SemaphoreType.DMA,
-        ],
-        compiler_params=remote_params(0),
-        name="gather_sources",
-    )(features, deg, rows, cols)
-
-    smem = spec(pltpu.SMEM)
     outs = (
         shaped((512, 256), BF16),
         shaped((512, 128), F32),
@@ -598,11 +571,19 @@
     results = pl.pallas_call(
         functools.partial(main_kernel, (512 * n_row * n_col) ** -0.5, n_row, n_col),
         out_shape=outs,
-        in_specs=[smem, smem, spec(), hbm, spec(), hbm, spec()],
+        in_specs=[spec(), spec(), spec(), hbm, spec(), hbm, spec()],
         out_specs=(spec(), spec(), spec()),
         scratch_shapes=[
+            pltpu.SMEM((8, SLOTS), I32),
+            pltpu.SMEM((8, SLOTS), I32),
+            VMEM((8, SLOTS), I32),
+            VMEM((8, SLOTS), I32),
+            VMEM(block, F32),
+            VMEM(block, F32),
             VMEM((4, 128), I32),
             VMEM((4, 128), I32),
+            VMEM((n_ct, 128, 128), BF16),
+            VMEM(block, BF16),
             VMEM((776, 16, 128), I32),
             VMEM((128, 128), F32),
             VMEM((EMPTY + 8, 128, 128), F32),
@@ -614,11 +595,17 @@
             VMEM((8,) + block, BF16),
             VMEM((7,) + block, BF16),
             VMEM((7,) + block, BF16),
+            VMEM(block, F32),
+            VMEM((4, 128, 256), F32),
             VMEM((128, 256), F32),
             VMEM((n_row, 8, 256), F32),
             VMEM((8, 256), F32),
             VMEM((n_col, 8, 256), F32),
             VMEM((128, 256), F32),
+            dma(16),
+            dma(16),
+            dma(16),
+            dma(16),
             dma(16),
             dma(16),
             dma(16),
@@ -636,10 +623,11 @@
             pltpu.SemaphoreType.DMA,
             pltpu.SemaphoreType.DMA,
             dma(2),
+            dma(2),
         ],
-        compiler_params=remote_params(1),
+        compiler_params=remote_params(0),
         name="layer",
-    )(fwd_list, bwd_list, gathered, masks, weight, deg, cotangent)
+    )(rows, cols, features, masks, weight, deg, cotangent)
     return pl.pallas_call(
         hand_on_kernel,
         out_shape=outs,

time: 93.4 us -> 87.7 us (0.939)
  Pallas kernels: 92.6 us -> 86.9 us
    pallas_call x1 -> x0, Pallas kernels: 20.2 us -> none  [body(): pl.pallas_call(gather_kernel, out_shape=(shaped((n_ct, 128, 128), BF16),...]
    pallas_call x1, Pallas kernels: 70.5 us -> 85 us  [body(): pl.pallas_call(functools.partial(main_kernel, (512 * n_row * n_col) ** (-...]
where the time goes in v5:
time: 87.7 us; the launch traced here: 87.6 us
  Pallas kernels  86.9 us (99%)
    pallas_call x1, Pallas kernels, body(): pl.pallas_call(functools.partial(main_kernel, (512 * n_row * n_col) ** (-...  85 us
    pallas_call x1, Pallas kernels, body(): pl.pallas_call(hand_on_kernel, out_shape=outs, in_specs=[spec()] * 3, out...  1.91 us

profile of v5, /device:TPU:1, one launch (start us, length us, event | category | flops | bytes accessed | tf_op | source)
XLA Modules:
  0.0 87.6 jit_solution(16014446593239604280)
XLA Ops:
  0.6 85.0 %layer.1 = (bf16[512,256]{1,0:T(8,128)(2,1)}, f32[512,128]{1,0:T(8,128)}, f32[128,256]{1,0:T(8,128)}) custom-call(s32[1,768]{1,0:T(1,128)} %bitcast.6, s32[1,768]{1,0:T(1,128)} %bitcast.7, bf16[512,128]{1,0:T(8,128)(2,1)} %feat.1, s32[768,16,128]{2,1,0:T(8,128)} %bitcast.4, bf16[128,256]{1,0:T(8,128)(2,1)} %weight.1, s32[128,4,128]{2,1,0:T(4,128)} %bitcast.5, ...), custom_call_target="tpu_custom_call" | custom-call | tf_op jit(solution)/shard_map/layer/pallas_call | solution.py:571
  85.7 1.9 %results.1 = (bf16[512,256]{1,0:T(8,128)(2,1)}, f32[512,128]{1,0:T(8,128)}, f32[128,256]{1,0:T(8,128)}) custom-call(bf16[512,256]{1,0:T(8,128)(2,1)} %get-tuple-element.6.a, f32[512,128]{1,0:T(8,128)} %get-tuple-element.7.b, f32[128,256]{1,0:T(8,128)} %get-tuple-element.8.c), custom_call_target="tpu_custom_call" | custom-call | tf_op jit(solution)/shard_map/results/pallas_call | solution.py:631

commit v6 on v5

--- a/solution.py
+++ b/solution.py
@@ -18,8 +18,8 @@
 CODE_BITS = ROW_BITS + COL_BITS
 FRESH = 24
 GROUP = 4
-FWD_ROUNDS, FWD_UNROLL = 8, 27
-BWD_ROUNDS, BWD_UNROLL = 8, 30
+FWD_ROUNDS, FWD_UNROLL = 4, 54
+BWD_ROUNDS, BWD_UNROLL = 4, 60
 EMPTY = BWD_ROUNDS * BWD_UNROLL
 BIG = 56 * 1024 * 1024
 
@@ -174,18 +174,16 @@
     pass_on(4, "x", "op")
     pass_on(5, "om", "op")
     wait(1, "om")
-    twin("x", "op", "om")
     yield
     wait(3, "xm")
     wait(4, "xp")
     wait(5, "o2")
     for t, to in enumerate(ROUTES[chunk]):
         pass_on(6 + t, to, SOURCE[to], t, 1)
-    twin("xm", "xp", "o2")
     yield
     for t in range(2):
         wait(6 + t, "x2", t, 1)
-    twin("x2")
+    twin("x", "op", "om", "xm", "xp", "o2", "x2")
     yield
     if place.core is not None:
         for i, name in enumerate(NAMES + ["o"]):
@@ -338,7 +336,8 @@
 
 
 def main_kernel(
-    scale, n_row, n_col, rows, cols, feat, masks, weight, degrees_all, cot, act, out, gw_out,
+    scale, n_row, n_col, rows_in, cols_in, feat_in, masks, weight_in, degrees_all, cot_in, act_out, out, gw_out,
+    rows, cols, feat, weight, cot, act,
     fwd, bwd, fwd_list, bwd_list, out_factor, back_factor, deg_t, deg_s, src, source, held, acc, run, targets, mine, staged_c, got_c, twin_out, from_twin, staged_r, got_r,
     agg_hold, grad_hold, gw, gw_got, gw_row, gw_col, gw_all,
     sa, ra, st, rt, sc, rc, sg, rg, s0, r0, sr, rr, s2, r2, s3, r3, s4, r4, mask_sem, own_sem, deg_sem, list_sem,
@@ -352,6 +351,9 @@
         pltpu.make_async_copy(degrees_all.at[row * n_col + col], deg_t, deg_sem.at[0]),
         pltpu.make_async_copy(degrees_all.at[col * n_row + row], deg_s, deg_sem.at[1]),
     ]
+    pairs = ((rows_in, rows), (cols_in, cols), (feat_in, feat), (weight_in, weight), (cot_in, cot))
+    for i, (x, y) in enumerate(pairs):
+        loads.append(pltpu.make_async_copy(x, y, deg_sem.at[2 + i]))
     for copy in loads:
         copy.start()
     barrier = pltpu.get_barrier_semaphore()
@@ -370,6 +372,7 @@
     run[EMPTY] = jnp.zeros((128, 128), F32)
     for copy in loads:
         copy.wait()
+    act_copy = pltpu.make_async_copy(act, act_out, deg_sem.at[7])
     back_factors = scale_sources(feat, deg_s, source)
     own = pltpu.make_async_copy(source, src.at[pl.ds(rows_place.index("o") * 4, 4)], own_sem)
     own.start()
@@ -438,6 +441,7 @@
         spread_start(cols_place, mine, targets, (sg, rg), None, c, sent)
     own = pltpu.make_async_copy(mine, targets.at[pl.ds(col * 4, 4)], own_sem)
     own.start()
+    act_copy.start()
     total = jnp.zeros((128, 256), F32)
     for t in range(4):
         t_hi, t_lo = split(agg_hold[t])
@@ -525,6 +529,7 @@
     for step in range(1, n_row):
         peer = lax.rem(row + n_row - step, n_row)
         landed(gw_all.at[pl.ds(peer * 8, 8)], r4.at[step])
+    act_copy.wait()
     gw_out[...] = gw_all[...]
 
 
@@ -571,9 +576,15 @@
     results = pl.pallas_call(
         functools.partial(main_kernel, (512 * n_row * n_col) ** -0.5, n_row, n_col),
         out_shape=outs,
-        in_specs=[spec(), spec(), spec(), hbm, spec(), hbm, spec()],
-        out_specs=(spec(), spec(), spec()),
+        in_specs=[hbm] * 7,
+        out_specs=(hbm, spec(), spec()),
         scratch_shapes=[
+            VMEM(rows.shape, I32),
+            VMEM(cols.shape, I32),
+            VMEM(features.shape, BF16),
+            VMEM(weight.shape, BF16),
+            VMEM(cotangent.shape, BF16),
+            VMEM(cotangent.shape, BF16),
             pltpu.SMEM((8, SLOTS), I32),
             pltpu.SMEM((8, SLOTS), I32),
             VMEM((8, SLOTS), I32),
@@ -622,7 +633,7 @@
             dma(n_row),
             pltpu.SemaphoreType.DMA,
             pltpu.SemaphoreType.DMA,
-            dma(2),
+            dma(8),
             dma(2),
         ],
         compiler_params=remote_params(0),

time: 87.7 us -> 84.7 us (0.966)
  Pallas kernels: 86.9 us -> 83.9 us
    pallas_call x1, Pallas kernels: 85 us -> 82 us  [body(): pl.pallas_call(functools.partial(main_kernel, (512 * n_row * n_col) ** (-...]
where the time goes in v6:
time: 84.7 us; the launch traced here: 84.6 us
  Pallas kernels  83.9 us (99%)
    pallas_call x1, Pallas kernels, body(): pl.pallas_call(functools.partial(main_kernel, (512 * n_row * n_col) ** (-...  82 us
    pallas_call x1, Pallas kernels, body(): pl.pallas_call(hand_on_kernel, out_shape=outs, in_specs=[spec()] * 3, out...  1.91 us

profile of v6, /device:TPU:1, one launch (start us, length us, event | category | flops | bytes accessed | tf_op | source)
XLA Modules:
  0.0 84.6 jit_solution(1262571957848682222)
XLA Ops:
  0.6 82.0 %layer.1 = (bf16[512,256]{1,0:T(8,128)(2,1)}, f32[512,128]{1,0:T(8,128)}, f32[128,256]{1,0:T(8,128)}) custom-call(s32[1,768]{1,0:T(1,128)} %bitcast.6, s32[1,768]{1,0:T(1,128)} %bitcast.7, bf16[512,128]{1,0:T(8,128)(2,1)} %feat_in.1, s32[768,16,128]{2,1,0:T(8,128)} %bitcast.4, bf16[128,256]{1,0:T(8,128)(2,1)} %weight_in.1, s32[128,4,128]{2,1,0:T(4,128)} %bitcast.5, ...), custom_call_target="tpu_custom_call" | custom-call | tf_op jit(solution)/shard_map/layer/pallas_call | solution.py:576
  82.7 1.9 %results.1 = (bf16[512,256]{1,0:T(8,128)(2,1)}, f32[512,128]{1,0:T(8,128)}, f32[128,256]{1,0:T(8,128)}) custom-call(bf16[512,256]{1,0:T(8,128)(2,1)} %get-tuple-element.6.a, f32[512,128]{1,0:T(8,128)} %get-tuple-element.7.b, f32[128,256]{1,0:T(8,128)} %get-tuple-element.8.c), custom_call_target="tpu_custom_call" | custom-call | tf_op jit(solution)/shard_map/results/pallas_call | solution.py:642

commit v7 on v6

--- a/solution.py
+++ b/solution.py
@@ -142,7 +142,7 @@
 def spread_start(place, mine, out, sems, twin_sems, chunk, sent):
     own = mine.at[pl.ds(2 * chunk, 2)]
     here = out.at[pl.ds(place.index("o") * 4 + 2 * chunk, 2)]
-    for i, to in enumerate(("x", "op", "om")):
+    for i, to in ((1, "op"), (2, "om"), (0, "x")):
         sent.append(send(own, here, sems, 8 * chunk + i, place.device(to)))
     if place.core is not None:
         sent.append(send(own, here, twin_sems, 8 * chunk + 7, place.device("twin")))
@@ -173,14 +173,14 @@
     wait(2, "op")
     pass_on(4, "x", "op")
     pass_on(5, "om", "op")
+    yield
+    for t, to in reversed(list(enumerate(ROUTES[chunk]))):
+        name = SOURCE[to]
+        wait({"xm": 3, "xp": 4, "o2": 5}[name], name)
+        pass_on(6 + t, to, name, t, 1)
+    yield
     wait(1, "om")
-    yield
-    wait(3, "xm")
-    wait(4, "xp")
-    wait(5, "o2")
-    for t, to in enumerate(ROUTES[chunk]):
-        pass_on(6 + t, to, SOURCE[to], t, 1)
-    yield
+    wait(*((4, "xp") if chunk == 0 else (3, "xm")))
     for t in range(2):
         wait(6 + t, "x2", t, 1)
     twin("x", "op", "om", "xm", "xp", "o2", "x2")

time: 84.7 us -> 84.4 us (level)
  no operation moved by 1% of the time
where the time goes in v7:
time: 84.4 us; the launch traced here: 84.2 us
  Pallas kernels  83.6 us (99%)
    pallas_call x1, Pallas kernels, body(): pl.pallas_call(functools.partial(main_kernel, (512 * n_row * n_col) ** (-...  81.7 us
    pallas_call x1, Pallas kernels, body(): pl.pallas_call(hand_on_kernel, out_shape=outs, in_specs=[spec()] * 3, out...  1.91 us

profile of v7, /device:TPU:1, one launch (start us, length us, event | category | flops | bytes accessed | tf_op | source)
XLA Modules:
  0.0 84.2 jit_solution(4196450111914805238)
XLA Ops:
  0.6 81.7 %layer.1 = (bf16[512,256]{1,0:T(8,128)(2,1)}, f32[512,128]{1,0:T(8,128)}, f32[128,256]{1,0:T(8,128)}) custom-call(s32[1,768]{1,0:T(1,128)} %bitcast.6, s32[1,768]{1,0:T(1,128)} %bitcast.7, bf16[512,128]{1,0:T(8,128)(2,1)} %feat_in.1, s32[768,16,128]{2,1,0:T(8,128)} %bitcast.4, bf16[128,256]{1,0:T(8,128)(2,1)} %weight_in.1, s32[128,4,128]{2,1,0:T(4,128)} %bitcast.5, ...), custom_call_target="tpu_custom_call" | custom-call | tf_op jit(solution)/shard_map/layer/pallas_call | solution.py:576
  82.3 1.9 %results.1 = (bf16[512,256]{1,0:T(8,128)(2,1)}, f32[512,128]{1,0:T(8,128)}, f32[128,256]{1,0:T(8,128)}) custom-call(bf16[512,256]{1,0:T(8,128)(2,1)} %get-tuple-element.6.a, f32[512,128]{1,0:T(8,128)} %get-tuple-element.7.b, f32[128,256]{1,0:T(8,128)} %get-tuple-element.8.c), custom_call_target="tpu_custom_call" | custom-call | tf_op jit(solution)/shard_map/results/pallas_call | solution.py:642

commit v8 on v7

--- a/solution.py
+++ b/solution.py
@@ -215,9 +215,9 @@
     stage("x2", 0)
     go(0, 0, 0, "x", both[:1])
     go(1, 0, 0, ("om", "op")[chunk], both[1:])
+    yield
     stage("om", 6)
     go(2, 6, 5, "om")
-    yield
     if chunk == 0:
         stage("xp", 1)
         go(3, 1, 1, "x")

time: 84.4 us -> 85.6 us (1.014)
  Pallas kernels: 83.6 us -> 84.8 us
    pallas_call x1, Pallas kernels: 81.7 us -> 82.9 us  [body(): pl.pallas_call(functools.partial(main_kernel, (512 * n_row * n_col) ** (-...]
where the time goes in v8:
time: 85.6 us; the launch traced here: 85.4 us
  Pallas kernels  84.8 us (99%)
    pallas_call x1, Pallas kernels, body(): pl.pallas_call(functools.partial(main_kernel, (512 * n_row * n_col) ** (-...  82.9 us
    pallas_call x1, Pallas kernels, body(): pl.pallas_call(hand_on_kernel, out_shape=outs, in_specs=[spec()] * 3, out...  1.91 us

profile of v8, /device:TPU:1, one launch (start us, length us, event | category | flops | bytes accessed | tf_op | source)
XLA Modules:
  0.0 85.4 jit_solution(4842190042964744347)
XLA Ops:
  0.6 82.9 %layer.1 = (bf16[512,256]{1,0:T(8,128)(2,1)}, f32[512,128]{1,0:T(8,128)}, f32[128,256]{1,0:T(8,128)}) custom-call(s32[1,768]{1,0:T(1,128)} %bitcast.6, s32[1,768]{1,0:T(1,128)} %bitcast.7, bf16[512,128]{1,0:T(8,128)(2,1)} %feat_in.1, s32[768,16,128]{2,1,0:T(8,128)} %bitcast.4, bf16[128,256]{1,0:T(8,128)(2,1)} %weight_in.1, s32[128,4,128]{2,1,0:T(4,128)} %bitcast.5, ...), custom_call_target="tpu_custom_call" | custom-call | tf_op jit(solution)/shard_map/layer/pallas_call | solution.py:576
  83.5 1.9 %results.1 = (bf16[512,256]{1,0:T(8,128)(2,1)}, f32[512,128]{1,0:T(8,128)}, f32[128,256]{1,0:T(8,128)}) custom-call(bf16[512,256]{1,0:T(8,128)(2,1)} %get-tuple-element.6.a, f32[512,128]{1,0:T(8,128)} %get-tuple-element.7.b, f32[128,256]{1,0:T(8,128)} %get-tuple-element.8.c), custom_call_target="tpu_custom_call" | custom-call | tf_op jit(solution)/shard_map/results/pallas_call | solution.py:642
